TPU v7x, 32 devices: a whole 2x2x4 slice. The times are simulated.
32 devices in a mesh: row: 16 (over z, x, core), rep: 2 (over y).
Axes of the slice: x: 2, y: 2, z: 4, core: 2. Of those that a mesh axis runs over, the one named last changes fastest.
Arguments:
- features: bfloat16 [32768, 256], P('row'), may hold values from -6 to 6
- adjacency: bfloat16 [256, 48, 128, 128], P('row', 'rep'), may hold values from 0 to 3, as said below
- columns: int32 [256, 48], P('row', 'rep'), may hold values from 0 to 255, as said below
- live: int32 [256], P('row'), may hold values from 0 to 48, as said below
- w_self: bfloat16 [256, 256], replicated, may hold values from -0.375 to 0.375
- w_neigh: bfloat16 [256, 256], replicated, may hold values from -4 to 4
- bias: float32 [256], replicated, may hold values from -3 to 3
Outputs:
- mixed: bfloat16 [32768, 256], P(('row', 'rep'))
Inputs may be any that keep to these rules, and one draw needn't show every extreme that they name: `adjacency`: edge weights are nonnegative; most entries are zero, and some nodes have no edges at all. `columns`: the column block of every slot of block row b lies in the block rows held by a row index at most 2 away from the one holding b (never outside the graph). Slots at or after live[b] are ignored; some block row uses all 48 slots.
All inputs are finite; a program needn't handle non-finite values.
Results may differ from a plain program's by a relative error of at most 0.0048.
Values may be sent and summed in bfloat16 or wider, within the bound.
No kernel may reach another device: no remote copies, remote signals or barrier semaphores. Data moves between devices by JAX's collectives and lax.ppermute only.
A program may use at most 64 MiB of HBM per device.

v0:
```python
import jax
import jax.numpy as jnp
from jax import lax
from jax.sharding import PartitionSpec as P

REACH = 2


def shifted(block, axis, distance):
    devices = range(lax.axis_size(axis))
    route = [(i - distance, i) for i in devices if i - distance in devices]
    return lax.ppermute(block, axis, route)


def tile_products(tiles, window_index, counts, first_slot, window):
    slot_total = tiles.shape[1]
    feature_width = window.shape[2]
    usable = jnp.clip(counts - first_slot, 0, slot_total)

    def one_row(row_item):
        row_tiles, row_index, row_count = row_item
        live_slots = jnp.arange(slot_total, dtype=jnp.int32) < row_count
        masked = jnp.where(live_slots[:, None, None], row_tiles, jnp.zeros((), row_tiles.dtype))
        source = window[row_index]
        running = jnp.einsum("sij,sjf->if", masked, source, preferred_element_type=jnp.float32)
        degree = jnp.sum(masked, axis=(0, 2), dtype=jnp.float32)
        return (running, degree)

    totals, degrees = lax.map(one_row, (tiles, window_index, usable))
    return (totals.reshape(-1, feature_width), degrees.reshape(-1))


def local(features, adjacency, columns, live, w_self, w_neigh, bias):
    feature_width = features.shape[1]
    tile_edge = adjacency.shape[2]
    own_blocks = features.shape[0] // tile_edge
    own_feats = features.reshape(own_blocks, tile_edge, feature_width)
    row_place = lax.axis_index("row")
    replica = lax.axis_index("rep")
    sharers = lax.axis_size("rep")
    nearby = {0: own_feats}
    for offset in range(-REACH, REACH + 1):
        if offset != 0:
            nearby[offset] = shifted(own_feats, "row", -offset)
    window = jnp.concatenate([nearby[offset] for offset in range(-REACH, REACH + 1)], axis=0)
    window_index = (columns // own_blocks - row_place + REACH) * own_blocks + columns % own_blocks
    out_rows = own_blocks * tile_edge // sharers
    totals, degrees = tile_products(
        adjacency, window_index, live, replica * columns.shape[1], window
    )
    totals, degrees = (
        lax.psum_scatter(totals, "rep", scatter_dimension=0, tiled=True),
        lax.psum_scatter(degrees, "rep", scatter_dimension=0, tiled=True),
    )
    own_rows = lax.dynamic_slice_in_dim(features, replica * out_rows, out_rows, 0)
    neighbor_mean = (totals / jnp.maximum(degrees, 1.0)[:, None]).astype(jnp.bfloat16)
    summed = jnp.dot(own_rows, w_self, preferred_element_type=jnp.float32)
    summed = summed + jnp.dot(neighbor_mean, w_neigh, preferred_element_type=jnp.float32) + bias
    return jax.nn.relu(summed).astype(jnp.bfloat16)


def solution(mesh):
    placed = (P("row", None), P("row", "rep", None, None), P("row", "rep"), P("row"), P(), P(), P())
    return jax.shard_map(
        local, mesh=mesh, in_specs=placed, out_specs=P(("row", "rep"), None), check_vma=False
    )
```

profile of v0, /device:TPU:0, one launch (start us, length us, event | category | flops | bytes accessed | tf_op | source)
XLA Modules:
  0.0 255.5 jit_solution(12346463382553826951)
XLA Ops:
  6.5 5.9 %collective-permute-start = (bf16[16,128,256]{2,1,0:T(8,128)(2,1)}, bf16[16,128,256]{2,1,0:T(8,128)(2,1)}, u32[]{:S(2)}, u32[]{:S(2)}) collective-permute-start(bf16[16,128,256]{2,1,0:T(8,128)(2,1)} %bitcast.43), channel_id=1, source_target_pairs={{0,4},{2,6},{4,8},{6,10},{8,12},{10,14},{12,16},{14,18},{16,20},{1... | collective-permute-start | bytes 3145736 | tf_op jit(solution)/shard_map/ppermute | solution.py:12
  18.0 51.1 %collective-permute-done = bf16[16,128,256]{2,1,0:T(8,128)(2,1)} collective-permute-done((bf16[16,128,256]{2,1,0:T(8,128)(2,1)}, bf16[16,128,256]{2,1,0:T(8,128)(2,1)}, u32[]{:S(2)}, u32[]{:S(2)}) %collective-permute-start) | collective-permute-done | bytes 1048608 | tf_op jit(solution)/shard_map/ppermute | solution.py:12
  72.0 2.3 copy-done.1
  74.3 130.0 %while.12 = (s32[]{:T(128)}, f32[16,128,256]{2,1,0:T(8,128)}, f32[16,128]{1,0:T(8,128)S(1)}, s32[16]{0:T(128)S(1)}, bf16[16,24,128,128]{3,2,1,0:T(8,128)(2,1)}, ...) while((s32[]{:T(128)}, f32[16,128,256]{2,1,0:T(8,128)}, ...), condition=%wide.region_2.3_spmd, body=%wide.region_0.2_spmd.sunk | while | flops 202900448 | bytes 6429761 | solution.py:29
  74.3 3.2 %gather_fusion = bf16[24,128,256]{2,1,0:T(8,128)(2,1)S(1)} fusion(bf16[80,128,256]{2,1,0:T(8,128)(2,1)} %get-tuple-element.126, s32[1024]{0:T(1024)S(1)} %pad_clamp_fusion.2), kind=kCustom, calls=%fused_computation.clone.1 | custom fusion | bytes 3145824 | tf_op jit(solution)/shard_map/while/body/eval_jaxpr/gather | solution.py:24
  82.5 3.1 %gather_fusion = bf16[24,128,256]{2,1,0:T(8,128)(2,1)S(1)} fusion(bf16[80,128,256]{2,1,0:T(8,128)(2,1)} %get-tuple-element.126, s32[1024]{0:T(1024)S(1)} %pad_clamp_fusion.2), kind=kCustom, calls=%fused_computation.clone.1 | custom fusion | bytes 3145824 | tf_op jit(solution)/shard_map/while/body/eval_jaxpr/gather | solution.py:24
  90.6 3.1 %gather_fusion = bf16[24,128,256]{2,1,0:T(8,128)(2,1)S(1)} fusion(bf16[80,128,256]{2,1,0:T(8,128)(2,1)} %get-tuple-element.126, s32[1024]{0:T(1024)S(1)} %pad_clamp_fusion.2), kind=kCustom, calls=%fused_computation.clone.1 | custom fusion | bytes 3145824 | tf_op jit(solution)/shard_map/while/body/eval_jaxpr/gather | solution.py:24
  98.8 3.1 %gather_fusion = bf16[24,128,256]{2,1,0:T(8,128)(2,1)S(1)} fusion(bf16[80,128,256]{2,1,0:T(8,128)(2,1)} %get-tuple-element.126, s32[1024]{0:T(1024)S(1)} %pad_clamp_fusion.2), kind=kCustom, calls=%fused_computation.clone.1 | custom fusion | bytes 3145824 | tf_op jit(solution)/shard_map/while/body/eval_jaxpr/gather | solution.py:24
  106.9 3.1 %gather_fusion = bf16[24,128,256]{2,1,0:T(8,128)(2,1)S(1)} fusion(bf16[80,128,256]{2,1,0:T(8,128)(2,1)} %get-tuple-element.126, s32[1024]{0:T(1024)S(1)} %pad_clamp_fusion.2), kind=kCustom, calls=%fused_computation.clone.1 | custom fusion | bytes 3145824 | tf_op jit(solution)/shard_map/while/body/eval_jaxpr/gather | solution.py:24
  115.0 3.1 %gather_fusion = bf16[24,128,256]{2,1,0:T(8,128)(2,1)S(1)} fusion(bf16[80,128,256]{2,1,0:T(8,128)(2,1)} %get-tuple-element.126, s32[1024]{0:T(1024)S(1)} %pad_clamp_fusion.2), kind=kCustom, calls=%fused_computation.clone.1 | custom fusion | bytes 3145824 | tf_op jit(solution)/shard_map/while/body/eval_jaxpr/gather | solution.py:24
  123.1 3.1 %gather_fusion = bf16[24,128,256]{2,1,0:T(8,128)(2,1)S(1)} fusion(bf16[80,128,256]{2,1,0:T(8,128)(2,1)} %get-tuple-element.126, s32[1024]{0:T(1024)S(1)} %pad_clamp_fusion.2), kind=kCustom, calls=%fused_computation.clone.1 | custom fusion | bytes 3145824 | tf_op jit(solution)/shard_map/while/body/eval_jaxpr/gather | solution.py:24
  131.3 3.1 %gather_fusion = bf16[24,128,256]{2,1,0:T(8,128)(2,1)S(1)} fusion(bf16[80,128,256]{2,1,0:T(8,128)(2,1)} %get-tuple-element.126, s32[1024]{0:T(1024)S(1)} %pad_clamp_fusion.2), kind=kCustom, calls=%fused_computation.clone.1 | custom fusion | bytes 3145824 | tf_op jit(solution)/shard_map/while/body/eval_jaxpr/gather | solution.py:24
  139.4 3.1 %gather_fusion = bf16[24,128,256]{2,1,0:T(8,128)(2,1)S(1)} fusion(bf16[80,128,256]{2,1,0:T(8,128)(2,1)} %get-tuple-element.126, s32[1024]{0:T(1024)S(1)} %pad_clamp_fusion.2), kind=kCustom, calls=%fused_computation.clone.1 | custom fusion | bytes 3145824 | tf_op jit(solution)/shard_map/while/body/eval_jaxpr/gather | solution.py:24
  147.5 3.1 %gather_fusion = bf16[24,128,256]{2,1,0:T(8,128)(2,1)S(1)} fusion(bf16[80,128,256]{2,1,0:T(8,128)(2,1)} %get-tuple-element.126, s32[1024]{0:T(1024)S(1)} %pad_clamp_fusion.2), kind=kCustom, calls=%fused_computation.clone.1 | custom fusion | bytes 3145824 | tf_op jit(solution)/shard_map/while/body/eval_jaxpr/gather | solution.py:24
  155.6 3.1 %gather_fusion = bf16[24,128,256]{2,1,0:T(8,128)(2,1)S(1)} fusion(bf16[80,128,256]{2,1,0:T(8,128)(2,1)} %get-tuple-element.126, s32[1024]{0:T(1024)S(1)} %pad_clamp_fusion.2), kind=kCustom, calls=%fused_computation.clone.1 | custom fusion | bytes 3145824 | tf_op jit(solution)/shard_map/while/body/eval_jaxpr/gather | solution.py:24
  163.7 3.1 %gather_fusion = bf16[24,128,256]{2,1,0:T(8,128)(2,1)S(1)} fusion(bf16[80,128,256]{2,1,0:T(8,128)(2,1)} %get-tuple-element.126, s32[1024]{0:T(1024)S(1)} %pad_clamp_fusion.2), kind=kCustom, calls=%fused_computation.clone.1 | custom fusion | bytes 3145824 | tf_op jit(solution)/shard_map/while/body/eval_jaxpr/gather | solution.py:24
  171.8 3.1 %gather_fusion = bf16[24,128,256]{2,1,0:T(8,128)(2,1)S(1)} fusion(bf16[80,128,256]{2,1,0:T(8,128)(2,1)} %get-tuple-element.126, s32[1024]{0:T(1024)S(1)} %pad_clamp_fusion.2), kind=kCustom, calls=%fused_computation.clone.1 | custom fusion | bytes 3145824 | tf_op jit(solution)/shard_map/while/body/eval_jaxpr/gather | solution.py:24
  176.2 2.2 fusion.28
  180.0 3.1 %gather_fusion = bf16[24,128,256]{2,1,0:T(8,128)(2,1)S(1)} fusion(bf16[80,128,256]{2,1,0:T(8,128)(2,1)} %get-tuple-element.126, s32[1024]{0:T(1024)S(1)} %pad_clamp_fusion.2), kind=kCustom, calls=%fused_computation.clone.1 | custom fusion | bytes 3145824 | tf_op jit(solution)/shard_map/while/body/eval_jaxpr/gather | solution.py:24
  188.1 3.1 %gather_fusion = bf16[24,128,256]{2,1,0:T(8,128)(2,1)S(1)} fusion(bf16[80,128,256]{2,1,0:T(8,128)(2,1)} %get-tuple-element.126, s32[1024]{0:T(1024)S(1)} %pad_clamp_fusion.2), kind=kCustom, calls=%fused_computation.clone.1 | custom fusion | bytes 3145824 | tf_op jit(solution)/shard_map/while/body/eval_jaxpr/gather | solution.py:24
  196.2 3.1 %gather_fusion = bf16[24,128,256]{2,1,0:T(8,128)(2,1)S(1)} fusion(bf16[80,128,256]{2,1,0:T(8,128)(2,1)} %get-tuple-element.126, s32[1024]{0:T(1024)S(1)} %pad_clamp_fusion.2), kind=kCustom, calls=%fused_computation.clone.1 | custom fusion | bytes 3145824 | tf_op jit(solution)/shard_map/while/body/eval_jaxpr/gather | solution.py:24
  205.9 5.0 %all-reduce = f32[2048]{0:T(1024)S(1)} all-reduce(f32[2048]{0:T(1024)S(1)} %bitcast.50), channel_id=3, replica_groups=mesh['row'=16,'rep'=2] {'rep'}, use_global_device_ids=true, to_apply=%region_4.5.clone | all-reduce | flops 2048 | bytes 16384
  210.9 35.3 %reduce-scatter.2.cloned.1.call-done = f32[1024,256]{1,0:T(8,128)} async-done(((f32[2048,256]{1,0:T(8,128)}), f32[1024,256]{1,0:T(8,128)}) %reduce-scatter.2.cloned.1.call-update) | async-done | bytes 1048592 | tf_op jit(solution)/shard_map/reduce_scatter | solution.py:52
  246.2 2.4 fusion.7
  (142 shorter events, 86.1 us)
Async XLA Ops:
  6.5 199.0 %copy-start = (bf16[256,256]{1,0:T(8,128)(2,1)S(1)}, bf16[256,256]{1,0:T(8,128)(2,1)}, u32[]{:S(2)}) copy-start(bf16[256,256]{1,0:T(8,128)(2,1)} %param.13) | copy-start | bytes 393220
  6.5 239.7 %reduce-scatter.2.cloned.1.call-start = ((), (), s32[]{:S(2)}) async-start(), calls=%async_computation.1 | async-start | bytes 3145728 | tf_op jit(solution)/shard_map/reduce_scatter | solution.py:52
  6.5 62.5 %collective-permute-start = (bf16[16,128,256]{2,1,0:T(8,128)(2,1)}, bf16[16,128,256]{2,1,0:T(8,128)(2,1)}, u32[]{:S(2)}, u32[]{:S(2)}) collective-permute-start(bf16[16,128,256]{2,1,0:T(8,128)(2,1)} %bitcast.43), channel_id=1, source_target_pairs={{0,4},{2,6},{4,8},{6,10},{8,12},{10,14},{12,16},{14,18},{16,20},{1... | collective-permute-start | bytes 3145736 | tf_op jit(solution)/shard_map/ppermute | solution.py:12
  12.5 57.9 %collective-permute-start.1 = (bf16[16,128,256]{2,1,0:T(8,128)(2,1)}, bf16[16,128,256]{2,1,0:T(8,128)(2,1)S(1)}, u32[]{:S(2)}, u32[]{:S(2)}) collective-permute-start(bf16[16,128,256]{2,1,0:T(8,128)(2,1)} %bitcast.44), channel_id=1, source_target_pairs={{0,2},{2,4},{4,6},{6,8},{8,10},{10,12},{12,14},{14,16},{16,18},{18... | collective-permute-start | bytes 3145736 | tf_op jit(solution)/shard_map/ppermute | solution.py:12
  14.0 57.8 %collective-permute-start.2 = (bf16[16,128,256]{2,1,0:T(8,128)(2,1)}, bf16[16,128,256]{2,1,0:T(8,128)(2,1)S(1)}, u32[]{:S(2)}, u32[]{:S(2)}) collective-permute-start(bf16[16,128,256]{2,1,0:T(8,128)(2,1)} %bitcast.45), channel_id=1, source_target_pairs={{2,0},{4,2},{6,4},{8,6},{10,8},{12,10},{14,12},{16,14},{18,16},{20... | collective-permute-start | bytes 3145736 | tf_op jit(solution)/shard_map/ppermute | solution.py:12
  15.3 56.5 %collective-permute-start.3 = (bf16[16,128,256]{2,1,0:T(8,128)(2,1)}, bf16[16,128,256]{2,1,0:T(8,128)(2,1)S(1)}, u32[]{:S(2)}, u32[]{:S(2)}) collective-permute-start(bf16[16,128,256]{2,1,0:T(8,128)(2,1)} %bitcast.46), channel_id=1, source_target_pairs={{4,0},{6,2},{8,4},{10,6},{12,8},{14,10},{16,12},{18,14},{20,16},{2... | collective-permute-start | bytes 3145736 | tf_op jit(solution)/shard_map/ppermute | solution.py:12
  71.9 2.3 copy-start.1
  74.2 130.1 %copy-start.5 = (u32[32]{0:T(128)S(1)}, u32[32]{0:T(128)}, u32[]{:S(2)}) copy-start(u32[32]{0:T(128)} %constant.75) | copy-start | bytes 388
  74.2 131.4 %copy-start.2 = (bf16[2048,256]{1,0:T(8,128)(2,1)S(1)}, bf16[2048,256]{1,0:T(8,128)(2,1)}, u32[]{:S(2)}) copy-start(bf16[2048,256]{1,0:T(8,128)(2,1)} %param.9) | copy-start | bytes 3145732
  74.2 172.0 %copy-start.3 = (bf16[256,256]{1,0:T(8,128)(2,1)S(1)}, bf16[256,256]{1,0:T(8,128)(2,1)}, u32[]{:S(2)}) copy-start(bf16[256,256]{1,0:T(8,128)(2,1)} %param.14) | copy-start | bytes 393220
  74.2 172.0 %copy-start.4 = (f32[256]{0:T(256)S(1)}, f32[256]{0:T(256)}, u32[]{:S(2)}) copy-start(f32[256]{0:T(256)} %param.15) | copy-start | bytes 3076
Sparse Core Ops, SparseCore 0:
  204.5 41.7 reduce-scatter.1
where the time goes:
time: 258 us; the launch traced here: 255 us
  waiting for transfers between devices  86.4 us (33%)
  local copies, waits for them, and re-layouts  66 us (26%)
  matrix products  38.1 us (15%)
  other arithmetic  35 us (14%)
  between operations  14.2 us (6%)
  starting transfers between devices  10 us (4%)
  blocking collectives  5.01 us (2%)
    ppermute x4, waiting for transfers between devices, shifted(): return lax.ppermute(block, axis, route)  51.1 us
    gather x16, local copies, waits for them, and re-layouts, one_row(): source = window[row_index]  50.2 us
    dot_general x16, matrix products, one_row(): jnp.einsum('sij,sjf->if', masked, source, preferred_element_type=jnp.floa...  35.4 us
    reduce_scatter x1, waiting for transfers between devices, local(): lax.psum_scatter(totals, 'rep', scatter_dimension=0, tiled=True)  35.3 us
    reduce_sum x16, other arithmetic, one_row(): degree = jnp.sum(masked, axis=(0, 2), dtype=jnp.float32)  23.3 us
    ppermute x4, starting transfers between devices, shifted(): return lax.ppermute(block, axis, route)  10 us
    lt x16, other arithmetic, one_row(): live_slots = jnp.arange(slot_total, dtype=jnp.int32) < row_count  10 us
    dynamic_slice x16, local copies, waits for them, and re-layouts, tile_products(): totals, degrees = lax.map(one_row, (tiles, window_index, usable))  9.59 us
  transfers between devices with their start and end apart: 5, of which 2 were waited for; matrix products, arithmetic and copies ran while one was open for 2% of the time, Pallas kernels for 0%

commit v1 on v0

v1 whole, which is shorter than its diff:
```python
import functools

import jax
import jax.numpy as jnp
from jax import lax
from jax.experimental import pallas as pl
from jax.experimental.pallas import tpu as pltpu
from jax.sharding import PartitionSpec as P

OWN, PAIR, CROSS, AHEAD, LAST = range(5)
SOURCES = 5
HALVES = 2
CUTS = ((1,), (1,))
OVER_CUTS = (2, 1)
GROUP = 2
VMEM_BYTES = 6 << 20
TINY = pl.CostEstimate(flops=0, bytes_accessed=0, transcendentals=0)


def after(x, *others):
    return lax.optimization_barrier((x, *others))[0]


def in_hbm(x):
    return pltpu.with_memory_space_constraint(x, pltpu.HBM)


def in_vmem(x):
    return pltpu.with_memory_space_constraint(x, pltpu.VMEM)


def piece_starts(h, rows):
    return [rows * sum(CUTS[h][:q]) // sum(CUTS[h]) for q in range(len(CUTS[h]) + 1)]


def swap_route(count, bit):
    return [(i, i ^ bit) for i in range(count)]


def ahead_route(count):
    return [(i, (i + 4) % count if i % 4 < 2 else (i - 4) % count) for i in range(count)]


def degree_kernel(own_part, usable, place, adj, degree, tiles, sems):
    rows = degree.shape[0]
    first = (place[0] if own_part else 1 - place[0]) * rows
    loads = [pltpu.make_async_copy(adj.at[first + i], tiles.at[i], sems.at[i]) for i in range(rows)]
    for load in loads:
        load.start()
    for i in range(rows):
        loads[i].wait()
        degree[i : i + 1, :] = degree_row(tiles, i, usable[first + i])


def degree_row(tiles, i, count):
    slots, edge = tiles.shape[1], tiles.shape[2]
    acc = jnp.zeros((edge, edge), jnp.float32)
    for s in range(slots):
        t = tiles[i, s]
        acc = acc + jnp.where(s < count, t, jnp.zeros_like(t)).astype(jnp.float32)
    return jnp.sum(acc.T, axis=0, keepdims=True)


def token_kernel(value, out):
    out[...] = jnp.full(out.shape, value[0], out.dtype)


def base_kernel(place, feats, w_self, bias, base, own, sem):
    half = own.shape[0]
    copy = pltpu.make_async_copy(feats.at[pl.ds(pl.multiple_of(place[0] * half, half), half)], own, sem)
    copy.start()
    copy.wait()
    base[...] = jnp.dot(own[...], w_self[...], preferred_element_type=jnp.float32) + bias[...]


def product_kernel(own_part, halves, resident, index, place, adj, feats, pair, *rest):
    counts = [2 + 2 * OVER_CUTS[h] for h in halves]
    pieces, rest = rest[: sum(counts)], rest[sum(counts) :]
    outs, rest = rest[: len(halves)], rest[len(halves) :]
    if resident:
        tiles = adj
        window, window_sems = rest
    else:
        tiles, window, window_sems, tile_sems = rest
    rows, slots, edge = tiles.shape[0], tiles.shape[1], tiles.shape[2]
    part = window.shape[2]
    shard = 2 * rows * edge
    first = (place[0] if own_part else 1 - place[0]) * rows

    copies, by_cross, by_ahead = [], [], []
    for k, h in enumerate(halves):

        def move(ref, at, m):
            return pltpu.make_async_copy(ref, window.at[k, pl.ds(at, ref.shape[0])], window_sems.at[k, m])

        columns = pl.ds(h * part, part)
        at, n = sum(counts[:k]), OVER_CUTS[h]
        cross, ahead = pieces[at : at + 2]
        cross_over, ahead_over = pieces[at + 2 : at + 2 + n], pieces[at + 2 + n : at + 2 + 2 * n]
        copies += [move(feats.at[:, columns], OWN * shard, 0), move(pair.at[:, columns], PAIR * shard, 1)]
        copies += [move(cross, CROSS * shard, 2), move(ahead, AHEAD * shard, 3)]
        for q in range(n):
            by_cross.append(move(cross_over[q], LAST * shard + q * (shard // n), 4 + q))
            by_ahead.append(move(ahead_over[q], LAST * shard + q * (shard // n), 4 + q))
    for copy in copies:
        copy.start()

    @pl.when(place[1] == 1)
    def _():
        for copy in by_cross:
            copy.start()

    @pl.when(place[1] == 0)
    def _():
        for copy in by_ahead:
            copy.start()

    if not resident:
        loads = [pltpu.make_async_copy(adj.at[first + i], tiles.at[i], tile_sems.at[i]) for i in range(rows)]
        for load in loads:
            load.start()
    for k in range(len(halves)):
        window[k, pl.ds(SOURCES * shard, edge), :] = jnp.zeros((edge, part), window.dtype)
    for copy in copies + by_cross:
        copy.wait()

    def block(at):
        cut = pl.ds(pl.multiple_of(at * edge, edge), edge)
        return jnp.concatenate([window[k, cut, :] for k in range(len(halves))], axis=1)

    for g in range(0, rows, GROUP):
        if not resident:
            for i in range(g, g + GROUP):
                loads[i].wait()
        for i in range(g, g + GROUP):
            acc = None
            for s in range(0, slots, 2):
                left = jnp.concatenate([tiles[i, s], tiles[i, s + 1]], axis=1)
                right = jnp.concatenate([block(index[first + i, s]), block(index[first + i, s + 1])], axis=0)
                d = jnp.dot(left, right, preferred_element_type=jnp.float32)
                acc = d if acc is None else acc + d
            for k, out in enumerate(outs):
                out[i * edge : (i + 1) * edge, :] = acc[:, k * part : (k + 1) * part].astype(out.dtype)


def final_kernel(degree, degree_far, base, own0, far0, own1, far1, w_neigh, out):
    rows, edge = degree.shape
    for i in range(rows):
        total = degree[i : i + 1, :] + degree_far[i : i + 1, :]
        scale = 1.0 / jnp.maximum(total, 1.0)
        column = jnp.broadcast_to(scale, (edge, edge)).T
        cut = pl.ds(i * edge, edge)
        mean = jnp.concatenate(
            [
                ((own0[cut, :] + far0[cut, :].astype(jnp.float32)) * column).astype(jnp.bfloat16),
                ((own1[cut, :] + far1[cut, :].astype(jnp.float32)) * column).astype(jnp.bfloat16),
            ],
            axis=1,
        )
        mixed = base[cut, :] + jnp.dot(mean, w_neigh[...], preferred_element_type=jnp.float32)
        out[cut, :] = jnp.maximum(mixed, 0.0).astype(out.dtype)


def local(features, adjacency, columns, live, w_self, w_neigh, bias):
    rows, width = features.shape
    block_rows, slots, edge, _ = adjacency.shape
    count = lax.axis_size("row")
    place = lax.axis_index("row")
    replica = lax.axis_index("rep")
    part = width // HALVES
    out_rows = rows // 2

    usable = jnp.clip(live - replica * slots, 0, slots)
    spot = jnp.reshape(replica, (1,)).astype(jnp.int32)

    offset = columns // block_rows - place
    to_pair = 1 - 2 * (place % 2)
    to_cross = jnp.where(place % 4 < 2, 2, -2)
    source = jnp.where(offset == to_pair, PAIR, jnp.where(offset == -to_pair, LAST, OWN))
    source = jnp.where(offset == to_cross, CROSS, jnp.where(offset == -to_cross, AHEAD, source))
    index = source * block_rows + columns % block_rows
    dead = jnp.arange(slots, dtype=jnp.int32)[None, :] >= usable[:, None]
    index = jnp.where(dead, SOURCES * block_rows, index).astype(jnp.int32)

    smem = pl.BlockSpec(memory_space=pltpu.SMEM)
    vmem = pl.BlockSpec(memory_space=pltpu.VMEM)
    hbm = pl.BlockSpec(memory_space=pltpu.HBM)
    params = pltpu.CompilerParams(vmem_limit_bytes=VMEM_BYTES)

    def cross_of(h, q):
        starts = piece_starts(h, rows)
        sent = features[starts[q] : starts[q + 1], h * part : (h + 1) * part]
        return lax.ppermute(sent, "row", swap_route(count, 2))

    cross = [[cross_of(h, q) for q in range(len(CUTS[h]))] for h in range(HALVES)]
    pair = lax.ppermute(features, "row", swap_route(count, 1))

    wide = pltpu.CompilerParams(vmem_limit_bytes=16 << 20)
    anyw = pl.BlockSpec(memory_space=pl.ANY)
    adjacency = in_hbm(adjacency)

    def ahead_of(p):
        return lax.ppermute(p, "row", ahead_route(count))

    def over(p):
        return lax.ppermute(p, "row", swap_route(count, 1))

    held = (block_rows // 2, slots, edge, edge)
    sems = pltpu.SemaphoreType.DMA((block_rows // 2,))

    def degree_of(own_part, usable):
        shape = jax.ShapeDtypeStruct((block_rows // 2, edge), jnp.float32)
        tiles = pltpu.VMEM(held, jnp.bfloat16)
        outs = pl.pallas_call(
            functools.partial(degree_kernel, own_part),
            out_shape=[shape] if own_part else [shape, tiles],
            in_specs=[smem, smem, hbm],
            out_specs=[vmem] if own_part else [vmem, vmem],
            scratch_shapes=[tiles, sems] if own_part else [sems],
            compiler_params=wide if own_part else params,
            cost_estimate=TINY,
        )(usable, spot, adjacency)
        return outs[0] if own_part else (outs[0], in_vmem(outs[1]))

    def product_of(own_part, halves, tiles, *args, resident=False):
        kind = jnp.float32 if own_part else jnp.bfloat16
        return pl.pallas_call(
            functools.partial(product_kernel, own_part, halves, resident),
            out_shape=[jax.ShapeDtypeStruct((out_rows, part), kind) for _ in halves],
            in_specs=[smem, smem, vmem if resident else hbm] + [anyw] * (2 + sum(2 + 2 * OVER_CUTS[h] for h in halves)),
            out_specs=[vmem] * len(halves),
            scratch_shapes=([] if resident else [pltpu.VMEM(held, jnp.bfloat16)])
            + [
                pltpu.VMEM((len(halves), SOURCES * rows + edge, part), jnp.bfloat16),
                pltpu.SemaphoreType.DMA((len(halves), 4 + max(OVER_CUTS))),
            ]
            + ([] if resident else [sems]),
            compiler_params=params if resident else wide,
            cost_estimate=TINY,
        )(index, spot2, tiles, *args)

    def rep_swap(x):
        return lax.ppermute(x, "rep", [(0, 1), (1, 0)])

    def base_of(features):
        return pl.pallas_call(
            base_kernel,
            out_shape=jax.ShapeDtypeStruct((out_rows, width), jnp.float32),
            in_specs=[smem, hbm, vmem, vmem],
            out_specs=vmem,
            scratch_shapes=[pltpu.VMEM((out_rows, width), jnp.bfloat16), pltpu.SemaphoreType.DMA],
            compiler_params=params,
            cost_estimate=TINY,
        )(spot, in_hbm(features), w_self, bias.reshape(1, width))

    def token_of(place):
        return pl.pallas_call(
            token_kernel,
            out_shape=jax.ShapeDtypeStruct((8, 128), jnp.int32),
            in_specs=[smem],
            out_specs=vmem,
            cost_estimate=pl.CostEstimate(flops=0, bytes_accessed=8 << 20, transcendentals=0),
        )(jnp.reshape(place, (1,)))

    takes_cross = (place % 4 == 1) | (place % 4 == 2)
    spot2 = jnp.stack([replica, takes_cross.astype(jnp.int32)])

    def halved(p, n):
        return [p[rows * q // n : rows * (q + 1) // n] for q in range(n)]

    (x0,), (x1,) = cross
    degree = degree_of(True, after(usable, spot2, index))
    degree_out, tiles_far = degree_of(False, after(usable, degree))
    base = base_of(after(features, degree))
    z0 = ahead_of(after(x0, degree_out, base))
    token = token_of(after(place, x1))
    z1 = ahead_of(x1)
    degree_far = rep_swap(degree_out)
    xo0 = [over(after(p, token)) for p in halved(x0, OVER_CUTS[0])]
    zo0 = [over(after(p, token)) for p in halved(z0, OVER_CUTS[0])]
    half0 = (x0, z0, *xo0, *zo0)
    (far0,) = product_of(False, (0,), tiles_far, after(features, degree_far), pair, *half0, resident=True)
    other0 = rep_swap(far0)
    xo1, zo1 = over(after(x1, far0)), over(after(z1, far0))
    half1 = (x1, z1, xo1, zo1)
    (far1,) = product_of(False, (1,), tiles_far, features, pair, *half1, resident=True)
    other1 = rep_swap(far1)
    nearby = product_of(True, (0, 1), adjacency, after(features, far1), pair, *half0, *half1)
    far = (other0, other1)

    return pl.pallas_call(
        final_kernel,
        out_shape=jax.ShapeDtypeStruct((out_rows, width), jnp.bfloat16),
        in_specs=[vmem] * 8,
        out_specs=vmem,
        compiler_params=params,
        cost_estimate=TINY,
    )(degree, degree_far, base, nearby[0], far[0], nearby[1], far[1], w_neigh)


def solution(mesh):
    placed = (P("row", None), P("row", "rep", None, None), P("row", "rep"), P("row"), P(), P(), P())
    return jax.shard_map(
        local, mesh=mesh, in_specs=placed, out_specs=P(("row", "rep"), None), check_vma=False
    )
```

time: 258 us -> 60.4 us (0.23)
  local copies, waits for them, and re-layouts: 66 us -> 1.35 us
  waiting for transfers between devices: 86.4 us -> 23.1 us
  matrix products: 38.1 us -> 0 us
  other arithmetic: 35 us -> 1.5 us
  Pallas kernels: 0 us -> 21.4 us
  between operations: 14.2 us -> 0.12 us
  blocking collectives: 5.01 us -> 0 us
  starting transfers between devices: 10 us -> 12.7 us
    gather x16 -> x0, local copies, waits for them, and re-layouts: 50.2 us -> none  [one_row(): source = window[row_index]]
    dot_general x18 -> x0, matrix products: 38.1 us -> none  [the longest x16 35.4 us: one_row(): jnp.einsum('sij,sjf->if', masked, source, preferred_element_type=jnp.floa...]
    reduce_scatter x1 -> x0, waiting for transfers between devices: 35.3 us -> none  [local(): lax.psum_scatter(totals, 'rep', scatter_dimension=0, tiled=True)]
    ppermute x4 -> x14, waiting for transfers between devices: 51.1 us -> 23.1 us  [the longest x2 11 us: cross_of(): return lax.ppermute(sent, 'row', swap_route(count, 2))]
    reduce_sum x16 -> x0, other arithmetic: 23.3 us -> none  [one_row(): degree = jnp.sum(masked, axis=(0, 2), dtype=jnp.float32)]
    pallas_call x0 -> x7, Pallas kernels: none -> 21.4 us  [the longest x3 11 us: product_of(): pl.pallas_call(functools.partial(product_kernel, own_part, halves, reside...]
    lt x16 -> x0, other arithmetic: 10 us -> none  [one_row(): live_slots = jnp.arange(slot_total, dtype=jnp.int32) < row_count]
    dynamic_slice x16 -> x0, local copies, waits for them, and re-layouts: 9.59 us -> none  [tile_products(): totals, degrees = lax.map(one_row, (tiles, window_index, usable))]
  transfers between devices with their start and end apart: 5 -> 14, of which waited for: 2 -> 9; matrix products, arithmetic and copies ran while one was open for 2% -> 5% of each run, Pallas kernels for 0% -> 34%
where the time goes in v1:
time: 60.4 us; the launch traced here: 60.2 us
  waiting for transfers between devices  23.1 us (38%)
  Pallas kernels  21.4 us (35%)
  starting transfers between devices  12.7 us (21%)
  other arithmetic  1.5 us (2%)
  local copies, waits for them, and re-layouts  1.35 us (2%)
    pallas_call x3, Pallas kernels, product_of(): pl.pallas_call(functools.partial(product_kernel, own_part, halves, reside...  11 us
    ppermute x2, waiting for transfers between devices, cross_of(): return lax.ppermute(sent, 'row', swap_route(count, 2))  11 us
    pallas_call x2, Pallas kernels, degree_of(): pl.pallas_call(functools.partial(degree_kernel, own_part), out_shape=[sha...  7.8 us
    ppermute x2, waiting for transfers between devices, ahead_of(): return lax.ppermute(p, 'row', ahead_route(count))  6.98 us
    ppermute x3, starting transfers between devices, rep_swap(): return lax.ppermute(x, 'rep', [(0, 1), (1, 0)])  4.62 us
    ppermute x2, starting transfers between devices, ahead_of(): return lax.ppermute(p, 'row', ahead_route(count))  3.91 us
    ppermute x3, waiting for transfers between devices, rep_swap(): return lax.ppermute(x, 'rep', [(0, 1), (1, 0)])  3.13 us
    ppermute x2, starting transfers between devices, cross_of(): return lax.ppermute(sent, 'row', swap_route(count, 2))  2.63 us
  transfers between devices with their start and end apart: 14, of which 9 were waited for; matrix products, arithmetic and copies ran while one was open for 5% of the time, Pallas kernels for 34%

profile of v1, /device:TPU:0, one launch (start us, length us, event | category | flops | bytes accessed | tf_op | source)
XLA Modules:
  0.0 60.2 jit_solution(7038373625743911810)
XLA Ops:
  0.5 1.3 %fusion.4 = (bf16[2048,128]{1,0:T(8,128)(2,1)S(1)}, bf16[2048,128]{1,0:T(8,128)(2,1)S(1)}) fusion(bf16[2048,256]{1,0:T(8,128)(2,1)} %feats.4), kind=kLoop, calls=%fused_computation.13 | loop fusion | bytes 2097152 | tf_op jit(solution)/shard_map/slice | solution.py:192
  1.7 2.6 %collective-permute-start.4 = (bf16[2048,128]{1,0:T(8,128)(2,1)S(1)}, bf16[2048,128]{1,0:T(8,128)(2,1)S(1)}, u32[]{:S(2)}, u32[]{:S(2)}) collective-permute-start(bf16[2048,128]{1,0:T(8,128)(2,1)S(1)} %get-tuple-element.39), channel_id=1, source_target_pairs={{0,4},{2,6},{4,0},{6,2},{8,12},{10,14},{12,8},{14,10},{16,20},{18,... | collective-permute-start | bytes 1572872 | tf_op jit(solution)/shard_map/ppermute | solution.py:193
  4.4 0.7 %subtract_clamp_fusion.usable = s32[16]{0:T(128)S(1)} fusion(s32[16]{0:T(128)} %param.10, s32[]{:T(128)S(6)} %mul.10), kind=kLoop, calls=%fused_computation.12 | loop fusion | flops 32 | bytes 132 | tf_op jit(solution)/shard_map/jit(clip)/min | solution.py:173
  5.0 0.8 %fusion.2.index = s32[16,24]{1,0:T(8,128)S(1)} fusion(s32[16,24]{1,0:T(8,128)} %param.9, s32[]{:T(128)S(6)} %neg.7, s32[]{:T(128)S(6)} %sub.26, s32[]{:T(128)S(6)} %neg.6, s32[]{:T(128)S(6)} %select_n.50, s32[]{:T(128)S(6)} %axis_index.25, s32[16]{0:T(128)S(1)} %subtract_clamp_fusion.usable), kind=kLoop, calls=%fused_computation.7 | loop fusion | flops 12288 | bytes 3156 | tf_op jit(solution)/shard_map/jit(_where)/select_n | solution.py:183
  5.9 3.9 %shard_map.73.degree = f32[8,128]{1,0:T(8,128)S(1)} custom-call(s32[16]{0:T(128)S(1)} %subtract_clamp_fusion.usable, s32[1]{0:T(128)} %bitcast.place, bf16[16,24,128,128]{3,2,1,0:T(8,128)(2,1)} %adj.5), custom_call_target="tpu_custom_call" | custom-call | tf_op jit(solution)/shard_map/pallas_call | solution.py:214
  9.8 3.9 %shard_map.74 = (f32[8,128]{1,0:T(8,128)S(1)}, bf16[8,24,128,128]{3,2,1,0:T(8,128)(2,1)S(1)}) custom-call(s32[16]{0:T(128)S(1)} %subtract_clamp_fusion.usable, s32[1]{0:T(128)} %bitcast.place, bf16[16,24,128,128]{3,2,1,0:T(8,128)(2,1)} %adj.5), custom_call_target="tpu_custom_call" | custom-call | tf_op jit(solution)/shard_map/pallas_call | solution.py:214
  13.7 1.4 %shard_map.75.base = f32[1024,256]{1,0:T(8,128)S(1)} custom-call(s32[1]{0:T(128)} %bitcast.place, bf16[2048,256]{1,0:T(8,128)(2,1)} %feats.4, bf16[256,256]{1,0:T(8,128)(2,1)S(1)} %copy-done.1, f32[1,256]{1,0:T(1,128)S(1)} %bitcast.4), custom_call_target="tpu_custom_call" | custom-call | tf_op jit(solution)/shard_map/pallas_call | solution.py:246
  15.1 2.0 %collective-permute-done.4.rest_0_ = bf16[2048,128]{1,0:T(8,128)(2,1)S(1)} collective-permute-done((bf16[2048,128]{1,0:T(8,128)(2,1)S(1)}, bf16[2048,128]{1,0:T(8,128)(2,1)S(1)}, u32[]{:S(2)}, u32[]{:S(2)}) %collective-permute-start.4) | collective-permute-done | bytes 524320 | tf_op jit(solution)/shard_map/ppermute | solution.py:193
  17.1 2.0 %collective-permute-start.5 = (bf16[2048,128]{1,0:T(8,128)(2,1)S(1)}, bf16[2048,128]{1,0:T(8,128)(2,1)S(1)}, u32[]{:S(2)}, u32[]{:S(2)}) collective-permute-start(bf16[2048,128]{1,0:T(8,128)(2,1)S(1)} %collective-permute-done.4.rest_0_), channel_id=1, source_target_pairs={{0,8},{2,10},{4,28},{6,30},{8,16},{10,18},{12,4},{14,6},{16,24},{1... | collective-permute-start | bytes 1572872 | tf_op jit(solution)/shard_map/ppermute | solution.py:203
  19.1 9.0 %collective-permute-done.2.rest_0_.rest_6_ = bf16[2048,128]{1,0:T(8,128)(2,1)S(1)} collective-permute-done((bf16[2048,128]{1,0:T(8,128)(2,1)S(1)}, bf16[2048,128]{1,0:T(8,128)(2,1)S(1)}, u32[]{:S(2)}, u32[]{:S(2)}) %collective-permute-start.2) | collective-permute-done | bytes 524320 | tf_op jit(solution)/shard_map/ppermute | solution.py:193
  28.2 1.9 %collective-permute-start.3 = (bf16[2048,128]{1,0:T(8,128)(2,1)S(1)}, bf16[2048,128]{1,0:T(8,128)(2,1)S(1)}, u32[]{:S(2)}, u32[]{:S(2)}) collective-permute-start(bf16[2048,128]{1,0:T(8,128)(2,1)S(1)} %collective-permute-done.2.rest_0_.rest_6_), channel_id=1, source_target_pairs={{0,8},{2,10},{4,28},{6,30},{8,16},{10,18},{12,4},{14,6},{16,24},{1... | collective-permute-start | bytes 1572872 | tf_op jit(solution)/shard_map/ppermute | solution.py:203
  30.1 1.5 %collective-permute-start = (f32[8,128]{1,0:T(8,128)S(1)}, f32[8,128]{1,0:T(8,128)S(1)}, u32[]{:S(2)}, u32[]{:S(2)}) collective-permute-start(f32[8,128]{1,0:T(8,128)S(1)} %get-tuple-element.24), channel_id=1, source_target_pairs={{0,1},{1,0},{2,3},{3,2},{4,5},{5,4},{6,7},{7,6},{8,9},{9,8},{10,11... | collective-permute-start | bytes 12296 | tf_op jit(solution)/shard_map/ppermute | solution.py:243
  31.6 0.9 %collective-permute-done.5.rest_1_ = bf16[2048,128]{1,0:T(8,128)(2,1)S(1)} collective-permute-done((bf16[2048,128]{1,0:T(8,128)(2,1)S(1)}, bf16[2048,128]{1,0:T(8,128)(2,1)S(1)}, u32[]{:S(2)}, u32[]{:S(2)}) %collective-permute-start.5) | collective-permute-done | bytes 524320 | tf_op jit(solution)/shard_map/ppermute | solution.py:203
  32.6 1.1 %collective-permute-done.degree_far = f32[8,128]{1,0:T(8,128)S(1)} collective-permute-done((f32[8,128]{1,0:T(8,128)S(1)}, f32[8,128]{1,0:T(8,128)S(1)}, u32[]{:S(2)}, u32[]{:S(2)}) %collective-permute-start) | collective-permute-done | bytes 4128 | tf_op jit(solution)/shard_map/ppermute | solution.py:243
  34.2 1.0 %collective-permute-done.8.rest_4_ = bf16[1024,128]{1,0:T(8,128)(2,1)S(1)} collective-permute-done((bf16[1024,128]{1,0:T(8,128)(2,1)S(1)}, bf16[1024,128]{1,0:T(8,128)(2,1)S(1)}, u32[]{:S(2)}, u32[]{:S(2)}) %collective-permute-start.8) | collective-permute-done | bytes 262176 | tf_op jit(solution)/shard_map/ppermute | solution.py:206
  35.6 2.9 %shard_map.76 = bf16[1024,128]{1,0:T(8,128)(2,1)S(1)} custom-call(s32[16,24]{1,0:T(8,128)S(1)} %fusion.2.index, s32[2]{0:T(128)S(1)} %pad_add_fusion.place, bf16[8,24,128,128]{3,2,1,0:T(8,128)(2,1)S(1)} %get-tuple-element.26.adj, bf16[2048,256]{1,0:T(8,128)(2,1)S(1)} %copy-done, bf16[2048,256]{1,0:T(8,128)(2,1)S(1)} %collective-permute-done.1.pair, ...), custom_call_target="tpu_custom_call" | custom-call | tf_op jit(solution)/shard_map/pallas_call | solution.py:227
  38.6 6.1 %collective-permute-done.3.rest_1_.rest_7_ = bf16[2048,128]{1,0:T(8,128)(2,1)S(1)} collective-permute-done((bf16[2048,128]{1,0:T(8,128)(2,1)S(1)}, bf16[2048,128]{1,0:T(8,128)(2,1)S(1)}, u32[]{:S(2)}, u32[]{:S(2)}) %collective-permute-start.3) | collective-permute-done | bytes 524320 | tf_op jit(solution)/shard_map/ppermute | solution.py:203
  45.2 1.5 %collective-permute-start.12 = (bf16[1024,128]{1,0:T(8,128)(2,1)S(1)}, bf16[1024,128]{1,0:T(8,128)(2,1)S(1)}, u32[]{:S(2)}, u32[]{:S(2)}) collective-permute-start(bf16[1024,128]{1,0:T(8,128)(2,1)S(1)} %shard_map.76), channel_id=1, source_target_pairs={{0,1},{1,0},{2,3},{3,2},{4,5},{5,4},{6,7},{7,6},{8,9},{9,8},{10,11... | collective-permute-start | bytes 786440 | tf_op jit(solution)/shard_map/ppermute | solution.py:243
  46.7 0.6 %collective-permute-done.11.rest_3_.rest_9_ = bf16[2048,128]{1,0:T(8,128)(2,1)S(1)} collective-permute-done((bf16[2048,128]{1,0:T(8,128)(2,1)S(1)}, bf16[2048,128]{1,0:T(8,128)(2,1)S(1)}, u32[]{:S(2)}, u32[]{:S(2)}) %collective-permute-start.11) | collective-permute-done | bytes 524320 | tf_op jit(solution)/shard_map/ppermute | solution.py:206
  47.3 2.9 %shard_map.77 = bf16[1024,128]{1,0:T(8,128)(2,1)S(1)} custom-call(s32[16,24]{1,0:T(8,128)S(1)} %fusion.2.index, s32[2]{0:T(128)S(1)} %pad_add_fusion.place, bf16[8,24,128,128]{3,2,1,0:T(8,128)(2,1)S(1)} %get-tuple-element.26.adj, bf16[2048,256]{1,0:T(8,128)(2,1)S(1)} %copy-done, bf16[2048,256]{1,0:T(8,128)(2,1)S(1)} %collective-permute-done.1.pair, ...), custom_call_target="tpu_custom_call" | custom-call | tf_op jit(solution)/shard_map/pallas_call | solution.py:227
  50.3 1.6 %collective-permute-start.13 = (bf16[1024,128]{1,0:T(8,128)(2,1)S(1)}, bf16[1024,128]{1,0:T(8,128)(2,1)S(1)}, u32[]{:S(2)}, u32[]{:S(2)}) collective-permute-start(bf16[1024,128]{1,0:T(8,128)(2,1)S(1)} %shard_map.77), channel_id=1, source_target_pairs={{0,1},{1,0},{2,3},{3,2},{4,5},{5,4},{6,7},{7,6},{8,9},{9,8},{10,11... | collective-permute-start | bytes 786440 | tf_op jit(solution)/shard_map/ppermute | solution.py:243
  51.9 5.1 %shard_map.78 = (f32[1024,128]{1,0:T(8,128)S(1)}, f32[1024,128]{1,0:T(8,128)S(1)}) custom-call(s32[16,24]{1,0:T(8,128)S(1)} %fusion.2.index, s32[2]{0:T(128)S(1)} %pad_add_fusion.place, bf16[16,24,128,128]{3,2,1,0:T(8,128)(2,1)} %adj.5, bf16[2048,256]{1,0:T(8,128)(2,1)S(1)} %copy-done, bf16[2048,256]{1,0:T(8,128)(2,1)S(1)} %collective-permute-done.1.pair, ...), custom_call_target="tpu_custom_call" | custom-call | tf_op jit(solution)/shard_map/pallas_call | solution.py:227
  57.0 2.0 %collective-permute-done.13.far1 = bf16[1024,128]{1,0:T(8,128)(2,1)S(1)} collective-permute-done((bf16[1024,128]{1,0:T(8,128)(2,1)S(1)}, bf16[1024,128]{1,0:T(8,128)(2,1)S(1)}, u32[]{:S(2)}, u32[]{:S(2)}) %collective-permute-start.13) | collective-permute-done | bytes 262176 | tf_op jit(solution)/shard_map/ppermute | solution.py:243
  59.0 1.2 %shard_map.79 = bf16[1024,256]{1,0:T(8,128)(2,1)} custom-call(f32[8,128]{1,0:T(8,128)S(1)} %shard_map.73.degree, f32[8,128]{1,0:T(8,128)S(1)} %collective-permute-done.degree_far, f32[1024,256]{1,0:T(8,128)S(1)} %shard_map.75.base, f32[1024,128]{1,0:T(8,128)S(1)} %get-tuple-element.37.own0, bf16[1024,128]{1,0:T(8,128)(2,1)S(1)} %collective-permute-done.12.far0, ...), custom_call_target="tpu_custom_call" | custom-call | tf_op jit(solution)/shard_map/pallas_call | solution.py:291
  (25 shorter events, 2.2 us)
Async XLA Ops:
  0.0 34.2 %collective-permute-start.1 = (bf16[2048,256]{1,0:T(8,128)(2,1)}, bf16[2048,256]{1,0:T(8,128)(2,1)S(1)}, u32[]{:S(2)}, u32[]{:S(2)}) collective-permute-start(bf16[2048,256]{1,0:T(8,128)(2,1)} %feats.4), channel_id=1, source_target_pairs={{0,2},{2,0},{4,6},{6,4},{8,10},{10,8},{12,14},{14,12},{16,18},{18,... | collective-permute-start | bytes 3145736 | tf_op jit(solution)/shard_map/ppermute | solution.py:196
  1.7 15.3 %collective-permute-start.4 = (bf16[2048,128]{1,0:T(8,128)(2,1)S(1)}, bf16[2048,128]{1,0:T(8,128)(2,1)S(1)}, u32[]{:S(2)}, u32[]{:S(2)}) collective-permute-start(bf16[2048,128]{1,0:T(8,128)(2,1)S(1)} %get-tuple-element.39), channel_id=1, source_target_pairs={{0,4},{2,6},{4,0},{6,2},{8,12},{10,14},{12,8},{14,10},{16,20},{18,... | collective-permute-start | bytes 1572872 | tf_op jit(solution)/shard_map/ppermute | solution.py:193
  4.3 23.8 %collective-permute-start.2 = (bf16[2048,128]{1,0:T(8,128)(2,1)S(1)}, bf16[2048,128]{1,0:T(8,128)(2,1)S(1)}, u32[]{:S(2)}, u32[]{:S(2)}) collective-permute-start(bf16[2048,128]{1,0:T(8,128)(2,1)S(1)} %get-tuple-element.40), channel_id=1, source_target_pairs={{0,4},{2,6},{4,0},{6,2},{8,12},{10,14},{12,8},{14,10},{16,20},{18,... | collective-permute-start | bytes 1572872 | tf_op jit(solution)/shard_map/ppermute | solution.py:193
  5.9 7.8 %copy-start.1 = (bf16[256,256]{1,0:T(8,128)(2,1)S(1)}, bf16[256,256]{1,0:T(8,128)(2,1)}, u32[]{:S(2)}) copy-start(bf16[256,256]{1,0:T(8,128)(2,1)} %w_self.1) | copy-start | bytes 393220
  5.9 7.8 %copy-start.3 = (f32[256]{0:T(256)S(1)}, f32[256]{0:T(256)}, u32[]{:S(2)}) copy-start(f32[256]{0:T(256)} %param.13) | copy-start | bytes 3076
  5.9 29.8 %copy-start = (bf16[2048,256]{1,0:T(8,128)(2,1)S(1)}, bf16[2048,256]{1,0:T(8,128)(2,1)}, u32[]{:S(2)}) copy-start(bf16[2048,256]{1,0:T(8,128)(2,1)} %feats.4) | copy-start | bytes 3145732
  17.1 15.5 %collective-permute-start.5 = (bf16[2048,128]{1,0:T(8,128)(2,1)S(1)}, bf16[2048,128]{1,0:T(8,128)(2,1)S(1)}, u32[]{:S(2)}, u32[]{:S(2)}) collective-permute-start(bf16[2048,128]{1,0:T(8,128)(2,1)S(1)} %collective-permute-done.4.rest_0_), channel_id=1, source_target_pairs={{0,8},{2,10},{4,28},{6,30},{8,16},{10,18},{12,4},{14,6},{16,24},{1... | collective-permute-start | bytes 1572872 | tf_op jit(solution)/shard_map/ppermute | solution.py:203
  28.1 5.6 %collective-permute-start.6 = (bf16[1024,128]{1,0:T(8,128)(2,1)S(1)}, bf16[1024,128]{1,0:T(8,128)(2,1)S(1)}, u32[]{:S(2)}, u32[]{:S(2)}) collective-permute-start(bf16[1024,128]{1,0:T(8,128)(2,1)S(1)} %get-tuple-element.30), channel_id=1, source_target_pairs={{0,2},{2,0},{4,6},{6,4},{8,10},{10,8},{12,14},{14,12},{16,18},{18,... | collective-permute-start | bytes 786440 | tf_op jit(solution)/shard_map/ppermute | solution.py:206
  28.2 16.4 %collective-permute-start.3 = (bf16[2048,128]{1,0:T(8,128)(2,1)S(1)}, bf16[2048,128]{1,0:T(8,128)(2,1)S(1)}, u32[]{:S(2)}, u32[]{:S(2)}) collective-permute-start(bf16[2048,128]{1,0:T(8,128)(2,1)S(1)} %collective-permute-done.2.rest_0_.rest_6_), channel_id=1, source_target_pairs={{0,8},{2,10},{4,28},{6,30},{8,16},{10,18},{12,4},{14,6},{16,24},{1... | collective-permute-start | bytes 1572872 | tf_op jit(solution)/shard_map/ppermute | solution.py:203
  30.1 3.6 %collective-permute-start = (f32[8,128]{1,0:T(8,128)S(1)}, f32[8,128]{1,0:T(8,128)S(1)}, u32[]{:S(2)}, u32[]{:S(2)}) collective-permute-start(f32[8,128]{1,0:T(8,128)S(1)} %get-tuple-element.24), channel_id=1, source_target_pairs={{0,1},{1,0},{2,3},{3,2},{4,5},{5,4},{6,7},{7,6},{8,9},{9,8},{10,11... | collective-permute-start | bytes 12296 | tf_op jit(solution)/shard_map/ppermute | solution.py:243
  32.5 1.7 %collective-permute-start.7 = (bf16[1024,128]{1,0:T(8,128)(2,1)S(1)}, bf16[1024,128]{1,0:T(8,128)(2,1)S(1)}, u32[]{:S(2)}, u32[]{:S(2)}) collective-permute-start(bf16[1024,128]{1,0:T(8,128)(2,1)S(1)} %get-tuple-element.31), channel_id=1, source_target_pairs={{0,2},{2,0},{4,6},{6,4},{8,10},{10,8},{12,14},{14,12},{16,18},{18,... | collective-permute-start | bytes 786440 | tf_op jit(solution)/shard_map/ppermute | solution.py:206
  33.7 1.5 %collective-permute-start.8 = (bf16[1024,128]{1,0:T(8,128)(2,1)S(1)}, bf16[1024,128]{1,0:T(8,128)(2,1)S(1)}, u32[]{:S(2)}, u32[]{:S(2)}) collective-permute-start(bf16[1024,128]{1,0:T(8,128)(2,1)S(1)} %get-tuple-element.32), channel_id=1, source_target_pairs={{0,2},{2,0},{4,6},{6,4},{8,10},{10,8},{12,14},{14,12},{16,18},{18,... | collective-permute-start | bytes 786440 | tf_op jit(solution)/shard_map/ppermute | solution.py:206
  33.7 1.9 %collective-permute-start.9 = (bf16[1024,128]{1,0:T(8,128)(2,1)S(1)}, bf16[1024,128]{1,0:T(8,128)(2,1)S(1)}, u32[]{:S(2)}, u32[]{:S(2)}) collective-permute-start(bf16[1024,128]{1,0:T(8,128)(2,1)S(1)} %get-tuple-element.33), channel_id=1, source_target_pairs={{0,2},{2,0},{4,6},{6,4},{8,10},{10,8},{12,14},{14,12},{16,18},{18,... | collective-permute-start | bytes 786440 | tf_op jit(solution)/shard_map/ppermute | solution.py:206
  38.6 20.4 %copy-start.2 = (bf16[256,256]{1,0:T(8,128)(2,1)S(1)}, bf16[256,256]{1,0:T(8,128)(2,1)}, u32[]{:S(2)}) copy-start(bf16[256,256]{1,0:T(8,128)(2,1)} %w_neigh.1) | copy-start | bytes 393220
  44.7 2.0 %collective-permute-start.10 = (bf16[2048,128]{1,0:T(8,128)(2,1)S(1)}, bf16[2048,128]{1,0:T(8,128)(2,1)S(1)}, u32[]{:S(2)}, u32[]{:S(2)}) collective-permute-start(bf16[2048,128]{1,0:T(8,128)(2,1)S(1)} %collective-permute-done.2.rest_0_.rest_6_), channel_id=1, source_target_pairs={{0,2},{2,0},{4,6},{6,4},{8,10},{10,8},{12,14},{14,12},{16,18},{18,... | collective-permute-start | bytes 1572872 | tf_op jit(solution)/shard_map/ppermute | solution.py:206
  44.7 2.7 %collective-permute-start.11 = (bf16[2048,128]{1,0:T(8,128)(2,1)S(1)}, bf16[2048,128]{1,0:T(8,128)(2,1)S(1)}, u32[]{:S(2)}, u32[]{:S(2)}) collective-permute-start(bf16[2048,128]{1,0:T(8,128)(2,1)S(1)} %collective-permute-done.3.rest_1_.rest_7_), channel_id=1, source_target_pairs={{0,2},{2,0},{4,6},{6,4},{8,10},{10,8},{12,14},{14,12},{16,18},{18,... | collective-permute-start | bytes 1572872 | tf_op jit(solution)/shard_map/ppermute | solution.py:206
  45.2 11.8 %collective-permute-start.12 = (bf16[1024,128]{1,0:T(8,128)(2,1)S(1)}, bf16[1024,128]{1,0:T(8,128)(2,1)S(1)}, u32[]{:S(2)}, u32[]{:S(2)}) collective-permute-start(bf16[1024,128]{1,0:T(8,128)(2,1)S(1)} %shard_map.76), channel_id=1, source_target_pairs={{0,1},{1,0},{2,3},{3,2},{4,5},{5,4},{6,7},{7,6},{8,9},{9,8},{10,11... | collective-permute-start | bytes 786440 | tf_op jit(solution)/shard_map/ppermute | solution.py:243
  50.3 8.7 %collective-permute-start.13 = (bf16[1024,128]{1,0:T(8,128)(2,1)S(1)}, bf16[1024,128]{1,0:T(8,128)(2,1)S(1)}, u32[]{:S(2)}, u32[]{:S(2)}) collective-permute-start(bf16[1024,128]{1,0:T(8,128)(2,1)S(1)} %shard_map.77), channel_id=1, source_target_pairs={{0,1},{1,0},{2,3},{3,2},{4,5},{5,4},{6,7},{7,6},{8,9},{9,8},{10,11... | collective-permute-start | bytes 786440 | tf_op jit(solution)/shard_map/ppermute | solution.py:243

commit v2 on v1

--- a/solution.py
+++ b/solution.py
@@ -10,8 +10,7 @@
 OWN, PAIR, CROSS, AHEAD, LAST = range(5)
 SOURCES = 5
 HALVES = 2
-CUTS = ((1,), (1,))
-OVER_CUTS = (2, 1)
+CUTS = (2, 1)
 GROUP = 2
 VMEM_BYTES = 6 << 20
 TINY = pl.CostEstimate(flops=0, bytes_accessed=0, transcendentals=0)
@@ -29,12 +28,13 @@
     return pltpu.with_memory_space_constraint(x, pltpu.VMEM)
 
 
-def piece_starts(h, rows):
-    return [rows * sum(CUTS[h][:q]) // sum(CUTS[h]) for q in range(len(CUTS[h]) + 1)]
-
-
 def swap_route(count, bit):
     return [(i, i ^ bit) for i in range(count)]
+
+
+def loop_route(count):
+    route = [(i, i + 4 if i % 4 < 2 else i - 4) for i in range(count)]
+    return [(i, j if 0 <= j < count else i ^ 2) for i, j in route]
 
 
 def ahead_route(count):
@@ -74,7 +74,7 @@
 
 
 def product_kernel(own_part, halves, resident, index, place, adj, feats, pair, *rest):
-    counts = [2 + 2 * OVER_CUTS[h] for h in halves]
+    counts = [4 * CUTS[h] for h in halves]
     pieces, rest = rest[: sum(counts)], rest[sum(counts) :]
     outs, rest = rest[: len(halves)], rest[len(halves) :]
     if resident:
@@ -94,14 +94,14 @@
             return pltpu.make_async_copy(ref, window.at[k, pl.ds(at, ref.shape[0])], window_sems.at[k, m])
 
         columns = pl.ds(h * part, part)
-        at, n = sum(counts[:k]), OVER_CUTS[h]
-        cross, ahead = pieces[at : at + 2]
-        cross_over, ahead_over = pieces[at + 2 : at + 2 + n], pieces[at + 2 + n : at + 2 + 2 * n]
+        at, n = sum(counts[:k]), CUTS[h]
+        cross, ahead, cross_over, ahead_over = (pieces[at + n * j : at + n * (j + 1)] for j in range(4))
         copies += [move(feats.at[:, columns], OWN * shard, 0), move(pair.at[:, columns], PAIR * shard, 1)]
-        copies += [move(cross, CROSS * shard, 2), move(ahead, AHEAD * shard, 3)]
         for q in range(n):
-            by_cross.append(move(cross_over[q], LAST * shard + q * (shard // n), 4 + q))
-            by_ahead.append(move(ahead_over[q], LAST * shard + q * (shard // n), 4 + q))
+            row = 0 if n == 1 else (place[0] if q == 0 else 1 - place[0]) * (shard // n)
+            copies += [move(cross[q], CROSS * shard + row, 2 + q), move(ahead[q], AHEAD * shard + row, 2 + n + q)]
+            by_cross.append(move(cross_over[q], LAST * shard + row, 2 + 2 * n + q))
+            by_ahead.append(move(ahead_over[q], LAST * shard + row, 2 + 2 * n + q))
     for copy in copies:
         copy.start()
 
@@ -187,12 +187,11 @@
     hbm = pl.BlockSpec(memory_space=pltpu.HBM)
     params = pltpu.CompilerParams(vmem_limit_bytes=VMEM_BYTES)
 
-    def cross_of(h, q):
-        starts = piece_starts(h, rows)
-        sent = features[starts[q] : starts[q + 1], h * part : (h + 1) * part]
+    def cross_of(sent):
         return lax.ppermute(sent, "row", swap_route(count, 2))
 
-    cross = [[cross_of(h, q) for q in range(len(CUTS[h]))] for h in range(HALVES)]
+    x0a = cross_of(lax.dynamic_slice(features, (replica * out_rows, 0), (out_rows, part)))
+    x1 = cross_of(features[:, part:])
     pair = lax.ppermute(features, "row", swap_route(count, 1))
 
     wide = pltpu.CompilerParams(vmem_limit_bytes=16 << 20)
@@ -227,12 +226,12 @@
         return pl.pallas_call(
             functools.partial(product_kernel, own_part, halves, resident),
             out_shape=[jax.ShapeDtypeStruct((out_rows, part), kind) for _ in halves],
-            in_specs=[smem, smem, vmem if resident else hbm] + [anyw] * (2 + sum(2 + 2 * OVER_CUTS[h] for h in halves)),
+            in_specs=[smem, smem, vmem if resident else hbm] + [anyw] * (2 + sum(4 * CUTS[h] for h in halves)),
             out_specs=[vmem] * len(halves),
             scratch_shapes=([] if resident else [pltpu.VMEM(held, jnp.bfloat16)])
             + [
                 pltpu.VMEM((len(halves), SOURCES * rows + edge, part), jnp.bfloat16),
-                pltpu.SemaphoreType.DMA((len(halves), 4 + max(OVER_CUTS))),
+                pltpu.SemaphoreType.DMA((len(halves), 2 + 3 * max(CUTS))),
             ]
             + ([] if resident else [sems]),
             compiler_params=params if resident else wide,
@@ -265,20 +264,15 @@
     takes_cross = (place % 4 == 1) | (place % 4 == 2)
     spot2 = jnp.stack([replica, takes_cross.astype(jnp.int32)])
 
-    def halved(p, n):
-        return [p[rows * q // n : rows * (q + 1) // n] for q in range(n)]
-
-    (x0,), (x1,) = cross
     degree = degree_of(True, after(usable, spot2, index))
-    degree_out, tiles_far = degree_of(False, after(usable, degree))
-    base = base_of(after(features, degree))
-    z0 = ahead_of(after(x0, degree_out, base))
-    token = token_of(after(place, x1))
-    z1 = ahead_of(x1)
+    z0a, x0b, xo0a = ahead_of(after(x0a, degree)), rep_swap(after(x0a, degree)), over(after(x0a, degree))
+    degree_out, tiles_far = degree_of(False, after(usable, xo0a))
+    z0b = rep_swap(after(z0a, degree_out))
+    base = base_of(after(features, degree_out))
+    z1 = lax.ppermute(after(x1, base), "row", loop_route(count))
     degree_far = rep_swap(degree_out)
-    xo0 = [over(after(p, token)) for p in halved(x0, OVER_CUTS[0])]
-    zo0 = [over(after(p, token)) for p in halved(z0, OVER_CUTS[0])]
-    half0 = (x0, z0, *xo0, *zo0)
+    xo0, zo0 = (xo0a, over(after(x0b, x1))), (over(after(z0a, x1)), over(after(z0b, x1)))
+    half0 = (x0a, x0b, z0a, z0b, *xo0, *zo0)
     (far0,) = product_of(False, (0,), tiles_far, after(features, degree_far), pair, *half0, resident=True)
     other0 = rep_swap(far0)
     xo1, zo1 = over(after(x1, far0)), over(after(z1, far0))

time: 60.4 us -> 54.3 us (0.90)
  waiting for transfers between devices: 23.1 us -> 18 us
  starting transfers between devices: 12.7 us -> 10.8 us
  local copies, waits for them, and re-layouts: 1.35 us -> 2.06 us
    ppermute x2, waiting for transfers between devices: 11 us -> 0.55 us  [cross_of(): return lax.ppermute(sent, 'row', swap_route(count, 2))]
    ppermute x3 -> x5, waiting for transfers between devices: 3.13 us -> 8.23 us  [rep_swap(): return lax.ppermute(x, 'rep', [(0, 1), (1, 0)])]
    ppermute x2 -> x1, waiting for transfers between devices: 6.98 us -> 3.58 us  [ahead_of(): return lax.ppermute(p, 'row', ahead_route(count))]
    ppermute x0 -> x1, waiting for transfers between devices: none -> 3.01 us  [local(): z1 = lax.ppermute(after(x1, base), 'row', loop_route(count))]
    ppermute x2 -> x1, starting transfers between devices: 3.91 us -> 2.03 us  [ahead_of(): return lax.ppermute(p, 'row', ahead_route(count))]
    dynamic_slice x0 -> x1, local copies, waits for them, and re-layouts: none -> 0.97 us  [local(): lax.dynamic_slice(features, (replica * out_rows, 0), (out_rows, part))]
    ppermute x6, waiting for transfers between devices: 2.02 us -> 2.66 us  [over(): return lax.ppermute(p, 'row', swap_route(count, 1))]
    ppermute x3 -> x5, starting transfers between devices: 4.62 us -> 4.95 us  [rep_swap(): return lax.ppermute(x, 'rep', [(0, 1), (1, 0)])]
  transfers between devices with their start and end apart: 14 -> 16, of which waited for: 9 -> 8; matrix products, arithmetic and copies ran while one was open for 5% -> 7% of each run, Pallas kernels for 34% -> 38%
where the time goes in v2:
time: 54.3 us; the launch traced here: 54 us
  Pallas kernels  21.5 us (40%)
  waiting for transfers between devices  18 us (33%)
  starting transfers between devices  10.8 us (20%)
  local copies, waits for them, and re-layouts  2.06 us (4%)
  other arithmetic  1.51 us (3%)
    pallas_call x3, Pallas kernels, product_of(): pl.pallas_call(functools.partial(product_kernel, own_part, halves, reside...  11.1 us
    ppermute x5, waiting for transfers between devices, rep_swap(): return lax.ppermute(x, 'rep', [(0, 1), (1, 0)])  8.23 us
    pallas_call x2, Pallas kernels, degree_of(): pl.pallas_call(functools.partial(degree_kernel, own_part), out_shape=[sha...  7.8 us
    ppermute x5, starting transfers between devices, rep_swap(): return lax.ppermute(x, 'rep', [(0, 1), (1, 0)])  4.95 us
    ppermute x1, waiting for transfers between devices, ahead_of(): return lax.ppermute(p, 'row', ahead_route(count))  3.58 us
    ppermute x1, waiting for transfers between devices, local(): z1 = lax.ppermute(after(x1, base), 'row', loop_route(count))  3.01 us
    ppermute x6, waiting for transfers between devices, over(): return lax.ppermute(p, 'row', swap_route(count, 1))  2.66 us
    ppermute x2, starting transfers between devices, cross_of(): return lax.ppermute(sent, 'row', swap_route(count, 2))  2.64 us
  transfers between devices with their start and end apart: 16, of which 8 were waited for; matrix products, arithmetic and copies ran while one was open for 7% of the time, Pallas kernels for 38%

profile of v2, /device:TPU:0, one launch (start us, length us, event | category | flops | bytes accessed | tf_op | source)
XLA Modules:
  0.0 54.0 jit_solution(13204997687494211672)
XLA Ops:
  0.5 1.0 %constant_dynamic-slice_fusion = bf16[1024,128]{1,0:T(8,128)(2,1)S(1)} fusion(bf16[2048,256]{1,0:T(8,128)(2,1)} %feats.4, s32[]{:T(128)S(6)} %select_n.61), kind=kLoop, calls=%fused_computation.13 | loop fusion | bytes 524292 | tf_op jit(solution)/shard_map/dynamic_slice | solution.py:193
  1.4 2.6 %collective-permute-start = (bf16[1024,128]{1,0:T(8,128)(2,1)S(1)}, bf16[1024,128]{1,0:T(8,128)(2,1)S(1)}, u32[]{:S(2)}, u32[]{:S(2)}) collective-permute-start(bf16[1024,128]{1,0:T(8,128)(2,1)S(1)} %constant_dynamic-slice_fusion), channel_id=1, source_target_pairs={{0,4},{2,6},{4,0},{6,2},{8,12},{10,14},{12,8},{14,10},{16,20},{18,... | collective-permute-start | bytes 786440 | tf_op jit(solution)/shard_map/ppermute | solution.py:191
  4.0 1.1 %slice.3 = bf16[2048,128]{1,0:T(8,128)(2,1)S(1)} slice(bf16[2048,256]{1,0:T(8,128)(2,1)} %feats.4), slice={[0:2048], [128:256]} | slice | bytes 1048576 | tf_op jit(solution)/shard_map/slice | solution.py:194
  5.2 0.7 %subtract_clamp_fusion.usable = s32[16]{0:T(128)S(1)} fusion(s32[16]{0:T(128)} %param.10, s32[]{:T(128)S(6)} %mul.13), kind=kLoop, calls=%fused_computation.12 | loop fusion | flops 32 | bytes 132 | tf_op jit(solution)/shard_map/jit(clip)/min | solution.py:173
  5.9 0.8 %fusion.2.index = s32[16,24]{1,0:T(8,128)S(1)} fusion(s32[16,24]{1,0:T(8,128)} %param.9, s32[]{:T(128)S(6)} %neg.7, s32[]{:T(128)S(6)} %sub.26, s32[]{:T(128)S(6)} %neg.6, s32[]{:T(128)S(6)} %select_n.53, s32[]{:T(128)S(6)} %axis_index.25, s32[16]{0:T(128)S(1)} %subtract_clamp_fusion.usable), kind=kLoop, calls=%fused_computation.7 | loop fusion | flops 12288 | bytes 3156 | tf_op jit(solution)/shard_map/jit(_where)/select_n | solution.py:183
  6.7 3.9 %shard_map.73.degree = f32[8,128]{1,0:T(8,128)S(1)} custom-call(s32[16]{0:T(128)S(1)} %subtract_clamp_fusion.usable, s32[1]{0:T(128)} %bitcast.place, bf16[16,24,128,128]{3,2,1,0:T(8,128)(2,1)} %adj.5), custom_call_target="tpu_custom_call" | custom-call | tf_op jit(solution)/shard_map/pallas_call | solution.py:213
  11.1 2.0 %collective-permute-start.7 = (bf16[1024,128]{1,0:T(8,128)(2,1)S(1)}, bf16[1024,128]{1,0:T(8,128)(2,1)S(1)}, u32[]{:S(2)}, u32[]{:S(2)}) collective-permute-start(bf16[1024,128]{1,0:T(8,128)(2,1)S(1)} %collective-permute-done.rest_0_), channel_id=1, source_target_pairs={{0,8},{2,10},{4,28},{6,30},{8,16},{10,18},{12,4},{14,6},{16,24},{1... | collective-permute-start | bytes 786440 | tf_op jit(solution)/shard_map/ppermute | solution.py:202
  13.2 1.5 %collective-permute-start.6 = (bf16[1024,128]{1,0:T(8,128)(2,1)S(1)}, bf16[1024,128]{1,0:T(8,128)(2,1)S(1)}, u32[]{:S(2)}, u32[]{:S(2)}) collective-permute-start(bf16[1024,128]{1,0:T(8,128)(2,1)S(1)} %collective-permute-done.rest_0_), channel_id=1, source_target_pairs={{0,1},{1,0},{2,3},{3,2},{4,5},{5,4},{6,7},{7,6},{8,9},{9,8},{10,11... | collective-permute-start | bytes 786440 | tf_op jit(solution)/shard_map/ppermute | solution.py:242
  14.7 3.9 %shard_map.74 = (f32[8,128]{1,0:T(8,128)S(1)}, bf16[8,24,128,128]{3,2,1,0:T(8,128)(2,1)S(1)}) custom-call(s32[16]{0:T(128)S(1)} %subtract_clamp_fusion.usable, s32[1]{0:T(128)} %bitcast.place, bf16[16,24,128,128]{3,2,1,0:T(8,128)(2,1)} %adj.5), custom_call_target="tpu_custom_call" | custom-call | tf_op jit(solution)/shard_map/pallas_call | solution.py:213
  18.6 3.6 %collective-permute-done.7.rest_2_ = bf16[1024,128]{1,0:T(8,128)(2,1)S(1)} collective-permute-done((bf16[1024,128]{1,0:T(8,128)(2,1)S(1)}, bf16[1024,128]{1,0:T(8,128)(2,1)S(1)}, u32[]{:S(2)}, u32[]{:S(2)}) %collective-permute-start.7) | collective-permute-done | bytes 262176 | tf_op jit(solution)/shard_map/ppermute | solution.py:202
  22.2 1.5 %collective-permute-start.8 = (bf16[1024,128]{1,0:T(8,128)(2,1)S(1)}, bf16[1024,128]{1,0:T(8,128)(2,1)S(1)}, u32[]{:S(2)}, u32[]{:S(2)}) collective-permute-start(bf16[1024,128]{1,0:T(8,128)(2,1)S(1)} %collective-permute-done.7.rest_2_), channel_id=1, source_target_pairs={{0,1},{1,0},{2,3},{3,2},{4,5},{5,4},{6,7},{7,6},{8,9},{9,8},{10,11... | collective-permute-start | bytes 786440 | tf_op jit(solution)/shard_map/ppermute | solution.py:242
  23.7 1.4 %shard_map.75.base = f32[1024,256]{1,0:T(8,128)S(1)} custom-call(s32[1]{0:T(128)} %bitcast.place, bf16[2048,256]{1,0:T(8,128)(2,1)} %feats.4, bf16[256,256]{1,0:T(8,128)(2,1)S(1)} %copy-done.1, f32[1,256]{1,0:T(1,128)S(1)} %bitcast.3), custom_call_target="tpu_custom_call" | custom-call | tf_op jit(solution)/shard_map/pallas_call | solution.py:245
  25.1 0.6 %collective-permute-start.2 = (f32[8,128]{1,0:T(8,128)S(1)}, f32[8,128]{1,0:T(8,128)S(1)}, u32[]{:S(2)}, u32[]{:S(2)}) collective-permute-start(f32[8,128]{1,0:T(8,128)S(1)} %get-tuple-element.25), channel_id=1, source_target_pairs={{0,1},{1,0},{2,3},{3,2},{4,5},{5,4},{6,7},{7,6},{8,9},{9,8},{10,11... | collective-permute-start | bytes 12296 | tf_op jit(solution)/shard_map/ppermute | solution.py:242
  25.7 4.6 %collective-permute-done.8.rest_3_ = bf16[1024,128]{1,0:T(8,128)(2,1)S(1)} collective-permute-done((bf16[1024,128]{1,0:T(8,128)(2,1)S(1)}, bf16[1024,128]{1,0:T(8,128)(2,1)S(1)}, u32[]{:S(2)}, u32[]{:S(2)}) %collective-permute-start.8) | collective-permute-done | bytes 262176 | tf_op jit(solution)/shard_map/ppermute | solution.py:242
  30.9 1.0 %collective-permute-done.10.rest_6_ = bf16[1024,128]{1,0:T(8,128)(2,1)S(1)} collective-permute-done((bf16[1024,128]{1,0:T(8,128)(2,1)S(1)}, bf16[1024,128]{1,0:T(8,128)(2,1)S(1)}, u32[]{:S(2)}, u32[]{:S(2)}) %collective-permute-start.10) | collective-permute-done | bytes 262176 | tf_op jit(solution)/shard_map/ppermute | solution.py:205
  32.3 3.0 %shard_map.76 = bf16[1024,128]{1,0:T(8,128)(2,1)S(1)} custom-call(s32[16,24]{1,0:T(8,128)S(1)} %fusion.2.index, s32[2]{0:T(128)S(1)} %pad_add_fusion.place, bf16[8,24,128,128]{3,2,1,0:T(8,128)(2,1)S(1)} %get-tuple-element.27.adj, bf16[2048,256]{1,0:T(8,128)(2,1)S(1)} %copy-done, bf16[2048,256]{1,0:T(8,128)(2,1)S(1)} %collective-permute-done.3.pair, ...), custom_call_target="tpu_custom_call" | custom-call | tf_op jit(solution)/shard_map/pallas_call | solution.py:226
  35.5 3.0 %collective-permute-done.5.rest_1_.rest_9_ = bf16[2048,128]{1,0:T(8,128)(2,1)S(1)} collective-permute-done((bf16[2048,128]{1,0:T(8,128)(2,1)S(1)}, bf16[2048,128]{1,0:T(8,128)(2,1)S(1)}, u32[]{:S(2)}, u32[]{:S(2)}) %collective-permute-start.5) | collective-permute-done | bytes 524320 | tf_op jit(solution)/shard_map/ppermute | solution.py:272
  38.5 0.6 %collective-permute-start.14 = (bf16[1024,128]{1,0:T(8,128)(2,1)S(1)}, bf16[1024,128]{1,0:T(8,128)(2,1)S(1)}, u32[]{:S(2)}, u32[]{:S(2)}) collective-permute-start(bf16[1024,128]{1,0:T(8,128)(2,1)S(1)} %shard_map.76), channel_id=1, source_target_pairs={{0,1},{1,0},{2,3},{3,2},{4,5},{5,4},{6,7},{7,6},{8,9},{9,8},{10,11... | collective-permute-start | bytes 786440 | tf_op jit(solution)/shard_map/ppermute | solution.py:242
  39.1 1.3 %collective-permute-done.13.rest_3_.rest_11_ = bf16[2048,128]{1,0:T(8,128)(2,1)S(1)} collective-permute-done((bf16[2048,128]{1,0:T(8,128)(2,1)S(1)}, bf16[2048,128]{1,0:T(8,128)(2,1)S(1)}, u32[]{:S(2)}, u32[]{:S(2)}) %collective-permute-start.13) | collective-permute-done | bytes 524320 | tf_op jit(solution)/shard_map/ppermute | solution.py:205
  40.4 3.0 %shard_map.77 = bf16[1024,128]{1,0:T(8,128)(2,1)S(1)} custom-call(s32[16,24]{1,0:T(8,128)S(1)} %fusion.2.index, s32[2]{0:T(128)S(1)} %pad_add_fusion.place, bf16[8,24,128,128]{3,2,1,0:T(8,128)(2,1)S(1)} %get-tuple-element.27.adj, bf16[2048,256]{1,0:T(8,128)(2,1)S(1)} %copy-done, bf16[2048,256]{1,0:T(8,128)(2,1)S(1)} %collective-permute-done.3.pair, ...), custom_call_target="tpu_custom_call" | custom-call | tf_op jit(solution)/shard_map/pallas_call | solution.py:226
  43.3 0.7 %collective-permute-start.15 = (bf16[1024,128]{1,0:T(8,128)(2,1)S(1)}, bf16[1024,128]{1,0:T(8,128)(2,1)S(1)}, u32[]{:S(2)}, u32[]{:S(2)}) collective-permute-start(bf16[1024,128]{1,0:T(8,128)(2,1)S(1)} %shard_map.77), channel_id=1, source_target_pairs={{0,1},{1,0},{2,3},{3,2},{4,5},{5,4},{6,7},{7,6},{8,9},{9,8},{10,11... | collective-permute-start | bytes 786440 | tf_op jit(solution)/shard_map/ppermute | solution.py:242
  44.0 5.2 %shard_map.78 = (f32[1024,128]{1,0:T(8,128)S(1)}, f32[1024,128]{1,0:T(8,128)S(1)}) custom-call(s32[16,24]{1,0:T(8,128)S(1)} %fusion.2.index, s32[2]{0:T(128)S(1)} %pad_add_fusion.place, bf16[16,24,128,128]{3,2,1,0:T(8,128)(2,1)} %adj.5, bf16[2048,256]{1,0:T(8,128)(2,1)S(1)} %copy-done, bf16[2048,256]{1,0:T(8,128)(2,1)S(1)} %collective-permute-done.3.pair, ...), custom_call_target="tpu_custom_call" | custom-call | tf_op jit(solution)/shard_map/pallas_call | solution.py:226
  49.3 3.5 %collective-permute-done.15.far1 = bf16[1024,128]{1,0:T(8,128)(2,1)S(1)} collective-permute-done((bf16[1024,128]{1,0:T(8,128)(2,1)S(1)}, bf16[1024,128]{1,0:T(8,128)(2,1)S(1)}, u32[]{:S(2)}, u32[]{:S(2)}) %collective-permute-start.15) | collective-permute-done | bytes 262176 | tf_op jit(solution)/shard_map/ppermute | solution.py:242
  52.8 1.2 %shard_map.79 = bf16[1024,256]{1,0:T(8,128)(2,1)} custom-call(f32[8,128]{1,0:T(8,128)S(1)} %shard_map.73.degree, f32[8,128]{1,0:T(8,128)S(1)} %collective-permute-done.2.degree_far, f32[1024,256]{1,0:T(8,128)S(1)} %shard_map.75.base, f32[1024,128]{1,0:T(8,128)S(1)} %get-tuple-element.37.own0, bf16[1024,128]{1,0:T(8,128)(2,1)S(1)} %collective-permute-done.14.far0, ...), custom_call_target="tpu_custom_call" | custom-call | tf_op jit(solution)/shard_map/pallas_call | solution.py:285
  (28 shorter events, 2.3 us)
Async XLA Ops:
  0.0 31.9 %collective-permute-start.3 = (bf16[2048,256]{1,0:T(8,128)(2,1)}, bf16[2048,256]{1,0:T(8,128)(2,1)S(1)}, u32[]{:S(2)}, u32[]{:S(2)}) collective-permute-start(bf16[2048,256]{1,0:T(8,128)(2,1)} %feats.4), channel_id=1, source_target_pairs={{0,2},{2,0},{4,6},{6,4},{8,10},{10,8},{12,14},{14,12},{16,18},{18,... | collective-permute-start | bytes 3145736 | tf_op jit(solution)/shard_map/ppermute | solution.py:195
  1.4 9.7 %collective-permute-start = (bf16[1024,128]{1,0:T(8,128)(2,1)S(1)}, bf16[1024,128]{1,0:T(8,128)(2,1)S(1)}, u32[]{:S(2)}, u32[]{:S(2)}) collective-permute-start(bf16[1024,128]{1,0:T(8,128)(2,1)S(1)} %constant_dynamic-slice_fusion), channel_id=1, source_target_pairs={{0,4},{2,6},{4,0},{6,2},{8,12},{10,14},{12,8},{14,10},{16,20},{18,... | collective-permute-start | bytes 786440 | tf_op jit(solution)/shard_map/ppermute | solution.py:191
  5.1 20.0 %collective-permute-start.4 = (bf16[2048,128]{1,0:T(8,128)(2,1)S(1)}, bf16[2048,128]{1,0:T(8,128)(2,1)S(1)}, u32[]{:S(2)}, u32[]{:S(2)}) collective-permute-start(bf16[2048,128]{1,0:T(8,128)(2,1)S(1)} %slice.3), channel_id=1, source_target_pairs={{0,4},{2,6},{4,0},{6,2},{8,12},{10,14},{12,8},{14,10},{16,20},{18,... | collective-permute-start | bytes 1572872 | tf_op jit(solution)/shard_map/ppermute | solution.py:191
  6.7 17.0 %copy-start.1 = (bf16[256,256]{1,0:T(8,128)(2,1)S(1)}, bf16[256,256]{1,0:T(8,128)(2,1)}, u32[]{:S(2)}) copy-start(bf16[256,256]{1,0:T(8,128)(2,1)} %w_self.1) | copy-start | bytes 393220
  6.7 17.0 %copy-start.3 = (f32[256]{0:T(256)S(1)}, f32[256]{0:T(256)}, u32[]{:S(2)}) copy-start(f32[256]{0:T(256)} %param.13) | copy-start | bytes 3076
  6.7 25.6 %copy-start = (bf16[2048,256]{1,0:T(8,128)(2,1)S(1)}, bf16[2048,256]{1,0:T(8,128)(2,1)}, u32[]{:S(2)}) copy-start(bf16[2048,256]{1,0:T(8,128)(2,1)} %feats.4) | copy-start | bytes 3145732
  11.1 3.6 %collective-permute-start.1 = (bf16[1024,128]{1,0:T(8,128)(2,1)S(1)}, bf16[1024,128]{1,0:T(8,128)(2,1)S(1)}, u32[]{:S(2)}, u32[]{:S(2)}) collective-permute-start(bf16[1024,128]{1,0:T(8,128)(2,1)S(1)} %collective-permute-done.rest_0_), channel_id=1, source_target_pairs={{0,2},{2,0},{4,6},{6,4},{8,10},{10,8},{12,14},{14,12},{16,18},{18,... | collective-permute-start | bytes 786440 | tf_op jit(solution)/shard_map/ppermute | solution.py:205
  11.1 11.0 %collective-permute-start.7 = (bf16[1024,128]{1,0:T(8,128)(2,1)S(1)}, bf16[1024,128]{1,0:T(8,128)(2,1)S(1)}, u32[]{:S(2)}, u32[]{:S(2)}) collective-permute-start(bf16[1024,128]{1,0:T(8,128)(2,1)S(1)} %collective-permute-done.rest_0_), channel_id=1, source_target_pairs={{0,8},{2,10},{4,28},{6,30},{8,16},{10,18},{12,4},{14,6},{16,24},{1... | collective-permute-start | bytes 786440 | tf_op jit(solution)/shard_map/ppermute | solution.py:202
  13.2 12.5 %collective-permute-start.6 = (bf16[1024,128]{1,0:T(8,128)(2,1)S(1)}, bf16[1024,128]{1,0:T(8,128)(2,1)S(1)}, u32[]{:S(2)}, u32[]{:S(2)}) collective-permute-start(bf16[1024,128]{1,0:T(8,128)(2,1)S(1)} %collective-permute-done.rest_0_), channel_id=1, source_target_pairs={{0,1},{1,0},{2,3},{3,2},{4,5},{5,4},{6,7},{7,6},{8,9},{9,8},{10,11... | collective-permute-start | bytes 786440 | tf_op jit(solution)/shard_map/ppermute | solution.py:242
  22.2 8.2 %collective-permute-start.8 = (bf16[1024,128]{1,0:T(8,128)(2,1)S(1)}, bf16[1024,128]{1,0:T(8,128)(2,1)S(1)}, u32[]{:S(2)}, u32[]{:S(2)}) collective-permute-start(bf16[1024,128]{1,0:T(8,128)(2,1)S(1)} %collective-permute-done.7.rest_2_), channel_id=1, source_target_pairs={{0,1},{1,0},{2,3},{3,2},{4,5},{5,4},{6,7},{7,6},{8,9},{9,8},{10,11... | collective-permute-start | bytes 786440 | tf_op jit(solution)/shard_map/ppermute | solution.py:242
  25.1 13.4 %collective-permute-start.5 = (bf16[2048,128]{1,0:T(8,128)(2,1)S(1)}, bf16[2048,128]{1,0:T(8,128)(2,1)S(1)}, u32[]{:S(2)}, u32[]{:S(2)}) collective-permute-start(bf16[2048,128]{1,0:T(8,128)(2,1)S(1)} %collective-permute-done.4.rest_0_.rest_8_), channel_id=1, source_target_pairs={{0,8},{2,10},{4,0},{6,2},{8,16},{10,18},{12,4},{14,6},{16,24},{18,... | collective-permute-start | bytes 1572872 | tf_op jit(solution)/shard_map/ppermute | solution.py:272
  25.1 5.3 %collective-permute-start.2 = (f32[8,128]{1,0:T(8,128)S(1)}, f32[8,128]{1,0:T(8,128)S(1)}, u32[]{:S(2)}, u32[]{:S(2)}) collective-permute-start(f32[8,128]{1,0:T(8,128)S(1)} %get-tuple-element.25), channel_id=1, source_target_pairs={{0,1},{1,0},{2,3},{3,2},{4,5},{5,4},{6,7},{7,6},{8,9},{9,8},{10,11... | collective-permute-start | bytes 12296 | tf_op jit(solution)/shard_map/ppermute | solution.py:242
  25.7 5.2 %collective-permute-start.9 = (bf16[1024,128]{1,0:T(8,128)(2,1)S(1)}, bf16[1024,128]{1,0:T(8,128)(2,1)S(1)}, u32[]{:S(2)}, u32[]{:S(2)}) collective-permute-start(bf16[1024,128]{1,0:T(8,128)(2,1)S(1)} %collective-permute-done.6.rest_1_), channel_id=1, source_target_pairs={{0,2},{2,0},{4,6},{6,4},{8,10},{10,8},{12,14},{14,12},{16,18},{18,... | collective-permute-start | bytes 786440 | tf_op jit(solution)/shard_map/ppermute | solution.py:205
  30.4 1.5 %collective-permute-start.10 = (bf16[1024,128]{1,0:T(8,128)(2,1)S(1)}, bf16[1024,128]{1,0:T(8,128)(2,1)S(1)}, u32[]{:S(2)}, u32[]{:S(2)}) collective-permute-start(bf16[1024,128]{1,0:T(8,128)(2,1)S(1)} %collective-permute-done.7.rest_2_), channel_id=1, source_target_pairs={{0,2},{2,0},{4,6},{6,4},{8,10},{10,8},{12,14},{14,12},{16,18},{18,... | collective-permute-start | bytes 786440 | tf_op jit(solution)/shard_map/ppermute | solution.py:205
  30.4 1.9 %collective-permute-start.11 = (bf16[1024,128]{1,0:T(8,128)(2,1)S(1)}, bf16[1024,128]{1,0:T(8,128)(2,1)S(1)}, u32[]{:S(2)}, u32[]{:S(2)}) collective-permute-start(bf16[1024,128]{1,0:T(8,128)(2,1)S(1)} %collective-permute-done.8.rest_3_), channel_id=1, source_target_pairs={{0,2},{2,0},{4,6},{6,4},{8,10},{10,8},{12,14},{14,12},{16,18},{18,... | collective-permute-start | bytes 786440 | tf_op jit(solution)/shard_map/ppermute | solution.py:205
  35.2 17.6 %copy-start.2 = (bf16[256,256]{1,0:T(8,128)(2,1)S(1)}, bf16[256,256]{1,0:T(8,128)(2,1)}, u32[]{:S(2)}) copy-start(bf16[256,256]{1,0:T(8,128)(2,1)} %w_neigh.1) | copy-start | bytes 393220
  35.2 3.9 %collective-permute-start.12 = (bf16[2048,128]{1,0:T(8,128)(2,1)S(1)}, bf16[2048,128]{1,0:T(8,128)(2,1)S(1)}, u32[]{:S(2)}, u32[]{:S(2)}) collective-permute-start(bf16[2048,128]{1,0:T(8,128)(2,1)S(1)} %collective-permute-done.4.rest_0_.rest_8_), channel_id=1, source_target_pairs={{0,2},{2,0},{4,6},{6,4},{8,10},{10,8},{12,14},{14,12},{16,18},{18,... | collective-permute-start | bytes 1572872 | tf_op jit(solution)/shard_map/ppermute | solution.py:205
  38.5 1.9 %collective-permute-start.13 = (bf16[2048,128]{1,0:T(8,128)(2,1)S(1)}, bf16[2048,128]{1,0:T(8,128)(2,1)S(1)}, u32[]{:S(2)}, u32[]{:S(2)}) collective-permute-start(bf16[2048,128]{1,0:T(8,128)(2,1)S(1)} %collective-permute-done.5.rest_1_.rest_9_), channel_id=1, source_target_pairs={{0,2},{2,0},{4,6},{6,4},{8,10},{10,8},{12,14},{14,12},{16,18},{18,... | collective-permute-start | bytes 1572872 | tf_op jit(solution)/shard_map/ppermute | solution.py:205
  38.5 10.8 %collective-permute-start.14 = (bf16[1024,128]{1,0:T(8,128)(2,1)S(1)}, bf16[1024,128]{1,0:T(8,128)(2,1)S(1)}, u32[]{:S(2)}, u32[]{:S(2)}) collective-permute-start(bf16[1024,128]{1,0:T(8,128)(2,1)S(1)} %shard_map.76), channel_id=1, source_target_pairs={{0,1},{1,0},{2,3},{3,2},{4,5},{5,4},{6,7},{7,6},{8,9},{9,8},{10,11... | collective-permute-start | bytes 786440 | tf_op jit(solution)/shard_map/ppermute | solution.py:242
  43.3 9.5 %collective-permute-start.15 = (bf16[1024,128]{1,0:T(8,128)(2,1)S(1)}, bf16[1024,128]{1,0:T(8,128)(2,1)S(1)}, u32[]{:S(2)}, u32[]{:S(2)}) collective-permute-start(bf16[1024,128]{1,0:T(8,128)(2,1)S(1)} %shard_map.77), channel_id=1, source_target_pairs={{0,1},{1,0},{2,3},{3,2},{4,5},{5,4},{6,7},{7,6},{8,9},{9,8},{10,11... | collective-permute-start | bytes 786440 | tf_op jit(solution)/shard_map/ppermute | solution.py:242

commit v3 on v2

--- a/solution.py
+++ b/solution.py
@@ -10,7 +10,8 @@
 OWN, PAIR, CROSS, AHEAD, LAST = range(5)
 SOURCES = 5
 HALVES = 2
-CUTS = (2, 1)
+OVER = (0, 3, 6, 8)
+ARGS = (8, 6)
 GROUP = 2
 VMEM_BYTES = 6 << 20
 TINY = pl.CostEstimate(flops=0, bytes_accessed=0, transcendentals=0)
@@ -74,8 +75,8 @@
 
 
 def product_kernel(own_part, halves, resident, index, place, adj, feats, pair, *rest):
-    counts = [4 * CUTS[h] for h in halves]
-    pieces, rest = rest[: sum(counts)], rest[sum(counts) :]
+    count = sum(ARGS[h] for h in halves)
+    pieces, rest = rest[:count], rest[count:]
     outs, rest = rest[: len(halves)], rest[len(halves) :]
     if resident:
         tiles = adj
@@ -94,26 +95,28 @@
             return pltpu.make_async_copy(ref, window.at[k, pl.ds(at, ref.shape[0])], window_sems.at[k, m])
 
         columns = pl.ds(h * part, part)
-        at, n = sum(counts[:k]), CUTS[h]
-        cross, ahead, cross_over, ahead_over = (pieces[at + n * j : at + n * (j + 1)] for j in range(4))
+        mine, pieces = pieces[: ARGS[h]], pieces[ARGS[h] :]
         copies += [move(feats.at[:, columns], OWN * shard, 0), move(pair.at[:, columns], PAIR * shard, 1)]
+        if h == 0:
+            starts = over_starts = [place[0] * (shard // 2), (1 - place[0]) * (shard // 2)]
+        else:
+            starts, over_starts = [0], [shard * e // 8 for e in OVER[:-1]]
+        n, m = len(starts), len(over_starts)
+        cross, ahead, cross_over, ahead_over = mine[:n], mine[n : 2 * n], mine[2 * n : 3 * n], mine[3 * n :]
         for q in range(n):
-            row = 0 if n == 1 else (place[0] if q == 0 else 1 - place[0]) * (shard // n)
-            copies += [move(cross[q], CROSS * shard + row, 2 + q), move(ahead[q], AHEAD * shard + row, 2 + n + q)]
-            by_cross.append(move(cross_over[q], LAST * shard + row, 2 + 2 * n + q))
-            by_ahead.append(move(ahead_over[q], LAST * shard + row, 2 + 2 * n + q))
+            copies += [move(cross[q], CROSS * shard + starts[q], 2 + q), move(ahead[q], AHEAD * shard + starts[q], 4 + q)]
+            by_cross.append(move(cross_over[q], LAST * shard + starts[q], 6 + q))
+        by_ahead += [move(ahead_over[q], LAST * shard + over_starts[q], 6 + q) for q in range(m)]
     for copy in copies:
         copy.start()
 
-    @pl.when(place[1] == 1)
-    def _():
-        for copy in by_cross:
-            copy.start()
-
-    @pl.when(place[1] == 0)
-    def _():
-        for copy in by_ahead:
-            copy.start()
+    sources = ((1, by_cross), (0, by_ahead))
+    for flag, some in sources:
+
+        @pl.when(place[1] == flag)
+        def _(some=some):
+            for copy in some:
+                copy.start()
 
     if not resident:
         loads = [pltpu.make_async_copy(adj.at[first + i], tiles.at[i], tile_sems.at[i]) for i in range(rows)]
@@ -121,8 +124,14 @@
             load.start()
     for k in range(len(halves)):
         window[k, pl.ds(SOURCES * shard, edge), :] = jnp.zeros((edge, part), window.dtype)
-    for copy in copies + by_cross:
+    for copy in copies:
         copy.wait()
+    for flag, some in sources:
+
+        @pl.when(place[1] == flag)
+        def _(some=some):
+            for copy in some:
+                copy.wait()
 
     def block(at):
         cut = pl.ds(pl.multiple_of(at * edge, edge), edge)
@@ -226,12 +235,12 @@
         return pl.pallas_call(
             functools.partial(product_kernel, own_part, halves, resident),
             out_shape=[jax.ShapeDtypeStruct((out_rows, part), kind) for _ in halves],
-            in_specs=[smem, smem, vmem if resident else hbm] + [anyw] * (2 + sum(4 * CUTS[h] for h in halves)),
+            in_specs=[smem, smem, vmem if resident else hbm] + [anyw] * (2 + sum(ARGS[h] for h in halves)),
             out_specs=[vmem] * len(halves),
             scratch_shapes=([] if resident else [pltpu.VMEM(held, jnp.bfloat16)])
             + [
                 pltpu.VMEM((len(halves), SOURCES * rows + edge, part), jnp.bfloat16),
-                pltpu.SemaphoreType.DMA((len(halves), 2 + 3 * max(CUTS))),
+                pltpu.SemaphoreType.DMA((len(halves), 6 + len(OVER))),
             ]
             + ([] if resident else [sems]),
             compiler_params=params if resident else wide,
@@ -264,21 +273,26 @@
     takes_cross = (place % 4 == 1) | (place % 4 == 2)
     spot2 = jnp.stack([replica, takes_cross.astype(jnp.int32)])
 
-    degree = degree_of(True, after(usable, spot2, index))
+    def loop_of(p):
+        return lax.ppermute(p, "row", loop_route(count))
+
+    degree = degree_of(True, usable)
     z0a, x0b, xo0a = ahead_of(after(x0a, degree)), rep_swap(after(x0a, degree)), over(after(x0a, degree))
-    degree_out, tiles_far = degree_of(False, after(usable, xo0a))
+    degree_out, tiles_far = degree_of(False, after(usable, xo0a, index, spot2))
     z0b = rep_swap(after(z0a, degree_out))
     base = base_of(after(features, degree_out))
-    z1 = lax.ppermute(after(x1, base), "row", loop_route(count))
+    z1 = loop_of(after(x1, base))
     degree_far = rep_swap(degree_out)
     xo0, zo0 = (xo0a, over(after(x0b, x1))), (over(after(z0a, x1)), over(after(z0b, x1)))
     half0 = (x0a, x0b, z0a, z0b, *xo0, *zo0)
     (far0,) = product_of(False, (0,), tiles_far, after(features, degree_far), pair, *half0, resident=True)
     other0 = rep_swap(far0)
-    xo1, zo1 = over(after(x1, far0)), over(after(z1, far0))
-    half1 = (x1, z1, xo1, zo1)
+    xo1 = over(after(x1, far0))
+    cuts = [rows * e // 8 for e in OVER]
+    zo1 = [over(after(z1, far0)[start:stop]) for start, stop in zip(cuts, cuts[1:])]
+    half1 = (x1, z1, xo1, *zo1)
     (far1,) = product_of(False, (1,), tiles_far, features, pair, *half1, resident=True)
-    other1 = rep_swap(far1)
+    other1 = rep_swap(after(far1, other0))
     nearby = product_of(True, (0, 1), adjacency, after(features, far1), pair, *half0, *half1)
     far = (other0, other1)
 

time: 54.3 us -> 52.1 us (0.959)
  waiting for transfers between devices: 18 us -> 11.2 us
  starting transfers between devices: 10.8 us -> 13.3 us
  Pallas kernels: 21.5 us -> 22.9 us
  local copies, waits for them, and re-layouts: 2.06 us -> 2.89 us
    ppermute x5, waiting for transfers between devices: 8.23 us -> 4.02 us  [rep_swap(): return lax.ppermute(x, 'rep', [(0, 1), (1, 0)])]
    ppermute x1, waiting for transfers between devices: 3.58 us -> 1.79 us  [ahead_of(): return lax.ppermute(p, 'row', ahead_route(count))]
    ppermute x5, starting transfers between devices: 4.95 us -> 6.58 us  [rep_swap(): return lax.ppermute(x, 'rep', [(0, 1), (1, 0)])]
    pallas_call x3, Pallas kernels: 11.1 us -> 12.5 us  [product_of(): pl.pallas_call(functools.partial(product_kernel, own_part, halves, reside...]
    ppermute x1, waiting for transfers between devices: 3.01 us -> 2.1 us  [loop_of(): return lax.ppermute(p, 'row', loop_route(count))]
    slice x1, local copies, waits for them, and re-layouts: 1.08 us -> 1.87 us  [local(): x1 = cross_of(features[:, part:])]
    ppermute x6 -> x8, starting transfers between devices: 0.69 us -> 1.39 us  [over(): return lax.ppermute(p, 'row', swap_route(count, 1))]
    ppermute x6 -> x8, waiting for transfers between devices: 2.66 us -> 2.67 us  [over(): return lax.ppermute(p, 'row', swap_route(count, 1))]
  transfers between devices with their start and end apart: 16 -> 18, of which waited for: 8 -> 8; matrix products, arithmetic and copies ran while one was open for 7% -> 7% of each run, Pallas kernels for 38% -> 42%
where the time goes in v3:
time: 52.1 us; the launch traced here: 51.8 us
  Pallas kernels  22.9 us (44%)
  starting transfers between devices  13.3 us (26%)
  waiting for transfers between devices  11.2 us (21%)
  local copies, waits for them, and re-layouts  2.89 us (6%)
  other arithmetic  1.5 us (3%)
    pallas_call x3, Pallas kernels, product_of(): pl.pallas_call(functools.partial(product_kernel, own_part, halves, reside...  12.5 us
    pallas_call x2, Pallas kernels, degree_of(): pl.pallas_call(functools.partial(degree_kernel, own_part), out_shape=[sha...  7.8 us
    ppermute x5, starting transfers between devices, rep_swap(): return lax.ppermute(x, 'rep', [(0, 1), (1, 0)])  6.58 us
    ppermute x5, waiting for transfers between devices, rep_swap(): return lax.ppermute(x, 'rep', [(0, 1), (1, 0)])  4.02 us
    ppermute x2, starting transfers between devices, cross_of(): return lax.ppermute(sent, 'row', swap_route(count, 2))  3.1 us
    ppermute x8, waiting for transfers between devices, over(): return lax.ppermute(p, 'row', swap_route(count, 1))  2.67 us
    ppermute x1, starting transfers between devices, ahead_of(): return lax.ppermute(p, 'row', ahead_route(count))  2.14 us
    ppermute x1, waiting for transfers between devices, loop_of(): return lax.ppermute(p, 'row', loop_route(count))  2.1 us
  transfers between devices with their start and end apart: 18, of which 8 were waited for; matrix products, arithmetic and copies ran while one was open for 7% of the time, Pallas kernels for 42%

profile of v3, /device:TPU:0, one launch (start us, length us, event | category | flops | bytes accessed | tf_op | source)
XLA Modules:
  0.0 51.8 jit_solution(9029453313294445496)
XLA Ops:
  0.0 1.0 %constant_dynamic-slice_fusion = bf16[1024,128]{1,0:T(8,128)(2,1)S(1)} fusion(bf16[2048,256]{1,0:T(8,128)(2,1)} %feats.4, s32[]{:T(128)S(6)} %select_n.51), kind=kLoop, calls=%fused_computation.13 | loop fusion | bytes 524292 | tf_op jit(solution)/shard_map/dynamic_slice | solution.py:202
  1.0 3.0 %collective-permute-start = (bf16[1024,128]{1,0:T(8,128)(2,1)S(1)}, bf16[1024,128]{1,0:T(8,128)(2,1)S(1)}, u32[]{:S(2)}, u32[]{:S(2)}) collective-permute-start(bf16[1024,128]{1,0:T(8,128)(2,1)S(1)} %constant_dynamic-slice_fusion), channel_id=1, source_target_pairs={{0,4},{2,6},{4,0},{6,2},{8,12},{10,14},{12,8},{14,10},{16,20},{18,... | collective-permute-start | bytes 786440 | tf_op jit(solution)/shard_map/ppermute | solution.py:200
  4.0 1.9 %slice.12 = bf16[2048,128]{1,0:T(8,128)(2,1)} slice(bf16[2048,256]{1,0:T(8,128)(2,1)} %feats.4), slice={[0:2048], [128:256]} | slice | bytes 1048576 | tf_op jit(solution)/shard_map/slice | solution.py:203
  5.9 0.7 %subtract_clamp_fusion.usable = s32[16]{0:T(128)S(1)} fusion(s32[16]{0:T(128)} %param.10, s32[]{:T(128)S(6)} %mul.13), kind=kLoop, calls=%fused_computation.12 | loop fusion | flops 32 | bytes 132 | tf_op jit(solution)/shard_map/jit(clip)/min | solution.py:182
  6.6 3.9 %shard_map.73.degree = f32[8,128]{1,0:T(8,128)S(1)} custom-call(s32[16]{0:T(128)S(1)} %subtract_clamp_fusion.usable, s32[1]{0:T(128)} %bitcast.place, bf16[16,24,128,128]{3,2,1,0:T(8,128)(2,1)} %adj.5), custom_call_target="tpu_custom_call" | custom-call | tf_op jit(solution)/shard_map/pallas_call | solution.py:222
  10.5 0.6 %collective-permute-done.rest_0_ = bf16[1024,128]{1,0:T(8,128)(2,1)S(1)} collective-permute-done((bf16[1024,128]{1,0:T(8,128)(2,1)S(1)}, bf16[1024,128]{1,0:T(8,128)(2,1)S(1)}, u32[]{:S(2)}, u32[]{:S(2)}) %collective-permute-start) | collective-permute-done | bytes 262176 | tf_op jit(solution)/shard_map/ppermute | solution.py:200
  11.1 2.1 %collective-permute-start.7 = (bf16[1024,128]{1,0:T(8,128)(2,1)S(1)}, bf16[1024,128]{1,0:T(8,128)(2,1)S(1)}, u32[]{:S(2)}, u32[]{:S(2)}) collective-permute-start(bf16[1024,128]{1,0:T(8,128)(2,1)S(1)} %collective-permute-done.rest_0_), channel_id=1, source_target_pairs={{0,8},{2,10},{4,28},{6,30},{8,16},{10,18},{12,4},{14,6},{16,24},{1... | collective-permute-start | bytes 786440 | tf_op jit(solution)/shard_map/ppermute | solution.py:211
  13.3 0.8 %fusion.2.index = s32[16,24]{1,0:T(8,128)S(1)} fusion(s32[16,24]{1,0:T(8,128)} %param.9, s32[]{:T(128)S(6)} %neg.7, s32[]{:T(128)S(6)} %sub.26, s32[]{:T(128)S(6)} %neg.6, s32[]{:T(128)S(6)} %select_n.54, s32[]{:T(128)S(6)} %axis_index.25, s32[16]{0:T(128)S(1)} %subtract_clamp_fusion.usable), kind=kLoop, calls=%fused_computation.7 | loop fusion | flops 12288 | bytes 3156 | tf_op jit(solution)/shard_map/jit(_where)/select_n | solution.py:192
  14.1 1.5 %collective-permute-start.6 = (bf16[1024,128]{1,0:T(8,128)(2,1)S(1)}, bf16[1024,128]{1,0:T(8,128)(2,1)S(1)}, u32[]{:S(2)}, u32[]{:S(2)}) collective-permute-start(bf16[1024,128]{1,0:T(8,128)(2,1)S(1)} %collective-permute-done.rest_0_), channel_id=1, source_target_pairs={{0,1},{1,0},{2,3},{3,2},{4,5},{5,4},{6,7},{7,6},{8,9},{9,8},{10,11... | collective-permute-start | bytes 786440 | tf_op jit(solution)/shard_map/ppermute | solution.py:251
  15.6 3.9 %shard_map.74 = (f32[8,128]{1,0:T(8,128)S(1)}, bf16[8,24,128,128]{3,2,1,0:T(8,128)(2,1)S(1)}) custom-call(s32[16]{0:T(128)S(1)} %subtract_clamp_fusion.usable, s32[1]{0:T(128)} %bitcast.place, bf16[16,24,128,128]{3,2,1,0:T(8,128)(2,1)} %adj.5), custom_call_target="tpu_custom_call" | custom-call | tf_op jit(solution)/shard_map/pallas_call | solution.py:222
  19.5 1.8 %collective-permute-done.7.rest_2_ = bf16[1024,128]{1,0:T(8,128)(2,1)S(1)} collective-permute-done((bf16[1024,128]{1,0:T(8,128)(2,1)S(1)}, bf16[1024,128]{1,0:T(8,128)(2,1)S(1)}, u32[]{:S(2)}, u32[]{:S(2)}) %collective-permute-start.7) | collective-permute-done | bytes 262176 | tf_op jit(solution)/shard_map/ppermute | solution.py:211
  21.3 1.5 %collective-permute-start.8 = (bf16[1024,128]{1,0:T(8,128)(2,1)S(1)}, bf16[1024,128]{1,0:T(8,128)(2,1)S(1)}, u32[]{:S(2)}, u32[]{:S(2)}) collective-permute-start(bf16[1024,128]{1,0:T(8,128)(2,1)S(1)} %collective-permute-done.7.rest_2_), channel_id=1, source_target_pairs={{0,1},{1,0},{2,3},{3,2},{4,5},{5,4},{6,7},{7,6},{8,9},{9,8},{10,11... | collective-permute-start | bytes 786440 | tf_op jit(solution)/shard_map/ppermute | solution.py:251
  22.9 1.4 %shard_map.75.base = f32[1024,256]{1,0:T(8,128)S(1)} custom-call(s32[1]{0:T(128)} %bitcast.place, bf16[2048,256]{1,0:T(8,128)(2,1)} %feats.4, bf16[256,256]{1,0:T(8,128)(2,1)S(1)} %copy-done.1, f32[1,256]{1,0:T(1,128)S(1)} %bitcast.3), custom_call_target="tpu_custom_call" | custom-call | tf_op jit(solution)/shard_map/pallas_call | solution.py:254
  24.3 0.6 %collective-permute-start.2 = (f32[8,128]{1,0:T(8,128)S(1)}, f32[8,128]{1,0:T(8,128)S(1)}, u32[]{:S(2)}, u32[]{:S(2)}) collective-permute-start(f32[8,128]{1,0:T(8,128)S(1)} %get-tuple-element.24), channel_id=1, source_target_pairs={{0,1},{1,0},{2,3},{3,2},{4,5},{5,4},{6,7},{7,6},{8,9},{9,8},{10,11... | collective-permute-start | bytes 12296 | tf_op jit(solution)/shard_map/ppermute | solution.py:251
  24.9 3.7 %collective-permute-done.8.rest_3_ = bf16[1024,128]{1,0:T(8,128)(2,1)S(1)} collective-permute-done((bf16[1024,128]{1,0:T(8,128)(2,1)S(1)}, bf16[1024,128]{1,0:T(8,128)(2,1)S(1)}, u32[]{:S(2)}, u32[]{:S(2)}) %collective-permute-start.8) | collective-permute-done | bytes 262176 | tf_op jit(solution)/shard_map/ppermute | solution.py:251
  29.1 1.0 %collective-permute-done.10.rest_6_ = bf16[1024,128]{1,0:T(8,128)(2,1)S(1)} collective-permute-done((bf16[1024,128]{1,0:T(8,128)(2,1)S(1)}, bf16[1024,128]{1,0:T(8,128)(2,1)S(1)}, u32[]{:S(2)}, u32[]{:S(2)}) %collective-permute-start.10) | collective-permute-done | bytes 262176 | tf_op jit(solution)/shard_map/ppermute | solution.py:214
  30.5 2.9 %shard_map.76 = bf16[1024,128]{1,0:T(8,128)(2,1)S(1)} custom-call(s32[16,24]{1,0:T(8,128)S(1)} %fusion.2.index, s32[2]{0:T(128)S(1)} %pad_add_fusion.place, bf16[8,24,128,128]{3,2,1,0:T(8,128)(2,1)S(1)} %get-tuple-element.26.adj, bf16[2048,256]{1,0:T(8,128)(2,1)S(1)} %copy-done, bf16[2048,256]{1,0:T(8,128)(2,1)S(1)} %collective-permute-done.3.pair, ...), custom_call_target="tpu_custom_call" | custom-call | tf_op jit(solution)/shard_map/pallas_call | solution.py:235
  33.6 1.5 %collective-permute-start.16 = (bf16[1024,128]{1,0:T(8,128)(2,1)S(1)}, bf16[1024,128]{1,0:T(8,128)(2,1)S(1)}, u32[]{:S(2)}, u32[]{:S(2)}) collective-permute-start(bf16[1024,128]{1,0:T(8,128)(2,1)S(1)} %shard_map.76), channel_id=1, source_target_pairs={{0,1},{1,0},{2,3},{3,2},{4,5},{5,4},{6,7},{7,6},{8,9},{9,8},{10,11... | collective-permute-start | bytes 786440 | tf_op jit(solution)/shard_map/ppermute | solution.py:251
  35.1 2.1 %collective-permute-done.5.rest_1_.rest_9_ = bf16[2048,128]{1,0:T(8,128)(2,1)S(1)} collective-permute-done((bf16[2048,128]{1,0:T(8,128)(2,1)S(1)}, bf16[2048,128]{1,0:T(8,128)(2,1)S(1)}, u32[]{:S(2)}, u32[]{:S(2)}) %collective-permute-start.5) | collective-permute-done | bytes 524320 | tf_op jit(solution)/shard_map/ppermute | solution.py:277
  38.0 1.3 %collective-permute-done.15.rest_5_.rest_13_ = bf16[512,128]{1,0:T(8,128)(2,1)S(1)} collective-permute-done((bf16[512,128]{1,0:T(8,128)(2,1)S(1)}, bf16[512,128]{1,0:T(8,128)(2,1)S(1)}, u32[]{:S(2)}, u32[]{:S(2)}) %collective-permute-start.15) | collective-permute-done | bytes 131104 | tf_op jit(solution)/shard_map/ppermute | solution.py:214
  39.2 3.6 %shard_map.77 = bf16[1024,128]{1,0:T(8,128)(2,1)S(1)} custom-call(s32[16,24]{1,0:T(8,128)S(1)} %fusion.2.index, s32[2]{0:T(128)S(1)} %pad_add_fusion.place, bf16[8,24,128,128]{3,2,1,0:T(8,128)(2,1)S(1)} %get-tuple-element.26.adj, bf16[2048,256]{1,0:T(8,128)(2,1)S(1)} %copy-done, bf16[2048,256]{1,0:T(8,128)(2,1)S(1)} %collective-permute-done.3.pair, ...), custom_call_target="tpu_custom_call" | custom-call | tf_op jit(solution)/shard_map/pallas_call | solution.py:235
  42.8 1.5 %collective-permute-start.17 = (bf16[1024,128]{1,0:T(8,128)(2,1)S(1)}, bf16[1024,128]{1,0:T(8,128)(2,1)S(1)}, u32[]{:S(2)}, u32[]{:S(2)}) collective-permute-start(bf16[1024,128]{1,0:T(8,128)(2,1)S(1)} %shard_map.77), channel_id=1, source_target_pairs={{0,1},{1,0},{2,3},{3,2},{4,5},{5,4},{6,7},{7,6},{8,9},{9,8},{10,11... | collective-permute-start | bytes 786440 | tf_op jit(solution)/shard_map/ppermute | solution.py:251
  44.3 6.0 %shard_map.78 = (f32[1024,128]{1,0:T(8,128)S(1)}, f32[1024,128]{1,0:T(8,128)S(1)}) custom-call(s32[16,24]{1,0:T(8,128)S(1)} %fusion.2.index, s32[2]{0:T(128)S(1)} %pad_add_fusion.place, bf16[16,24,128,128]{3,2,1,0:T(8,128)(2,1)} %adj.5, bf16[2048,256]{1,0:T(8,128)(2,1)S(1)} %copy-done, bf16[2048,256]{1,0:T(8,128)(2,1)S(1)} %collective-permute-done.3.pair, ...), custom_call_target="tpu_custom_call" | custom-call | tf_op jit(solution)/shard_map/pallas_call | solution.py:235
  50.7 1.2 %shard_map.79 = bf16[1024,256]{1,0:T(8,128)(2,1)} custom-call(f32[8,128]{1,0:T(8,128)S(1)} %shard_map.73.degree, f32[8,128]{1,0:T(8,128)S(1)} %collective-permute-done.2.degree_far, f32[1024,256]{1,0:T(8,128)S(1)} %shard_map.75.base, f32[1024,128]{1,0:T(8,128)S(1)} %get-tuple-element.36.own0, bf16[1024,128]{1,0:T(8,128)(2,1)S(1)} %collective-permute-done.16.far0, ...), custom_call_target="tpu_custom_call" | custom-call | tf_op jit(solution)/shard_map/pallas_call | solution.py:299
  (34 shorter events, 2.4 us)
Async XLA Ops:
  1.0 10.1 %collective-permute-start = (bf16[1024,128]{1,0:T(8,128)(2,1)S(1)}, bf16[1024,128]{1,0:T(8,128)(2,1)S(1)}, u32[]{:S(2)}, u32[]{:S(2)}) collective-permute-start(bf16[1024,128]{1,0:T(8,128)(2,1)S(1)} %constant_dynamic-slice_fusion), channel_id=1, source_target_pairs={{0,4},{2,6},{4,0},{6,2},{8,12},{10,14},{12,8},{14,10},{16,20},{18,... | collective-permute-start | bytes 786440 | tf_op jit(solution)/shard_map/ppermute | solution.py:200
  4.0 26.1 %collective-permute-start.3 = (bf16[2048,256]{1,0:T(8,128)(2,1)}, bf16[2048,256]{1,0:T(8,128)(2,1)S(1)}, u32[]{:S(2)}, u32[]{:S(2)}) collective-permute-start(bf16[2048,256]{1,0:T(8,128)(2,1)} %feats.4), channel_id=1, source_target_pairs={{0,2},{2,0},{4,6},{6,4},{8,10},{10,8},{12,14},{14,12},{16,18},{18,... | collective-permute-start | bytes 3145736 | tf_op jit(solution)/shard_map/ppermute | solution.py:204
  5.8 18.4 %collective-permute-start.4 = (bf16[2048,128]{1,0:T(8,128)(2,1)}, bf16[2048,128]{1,0:T(8,128)(2,1)S(1)}, u32[]{:S(2)}, u32[]{:S(2)}) collective-permute-start(bf16[2048,128]{1,0:T(8,128)(2,1)} %slice.12), channel_id=1, source_target_pairs={{0,4},{2,6},{4,0},{6,2},{8,12},{10,14},{12,8},{14,10},{16,20},{18,... | collective-permute-start | bytes 1572872 | tf_op jit(solution)/shard_map/ppermute | solution.py:200
  6.6 16.2 %copy-start.1 = (bf16[256,256]{1,0:T(8,128)(2,1)S(1)}, bf16[256,256]{1,0:T(8,128)(2,1)}, u32[]{:S(2)}) copy-start(bf16[256,256]{1,0:T(8,128)(2,1)} %w_self.1) | copy-start | bytes 393220
  6.6 16.3 %copy-start.3 = (f32[256]{0:T(256)S(1)}, f32[256]{0:T(256)}, u32[]{:S(2)}) copy-start(f32[256]{0:T(256)} %param.13) | copy-start | bytes 3076
  6.6 23.9 %copy-start = (bf16[2048,256]{1,0:T(8,128)(2,1)S(1)}, bf16[2048,256]{1,0:T(8,128)(2,1)}, u32[]{:S(2)}) copy-start(bf16[2048,256]{1,0:T(8,128)(2,1)} %feats.4) | copy-start | bytes 3145732
  11.1 10.2 %collective-permute-start.7 = (bf16[1024,128]{1,0:T(8,128)(2,1)S(1)}, bf16[1024,128]{1,0:T(8,128)(2,1)S(1)}, u32[]{:S(2)}, u32[]{:S(2)}) collective-permute-start(bf16[1024,128]{1,0:T(8,128)(2,1)S(1)} %collective-permute-done.rest_0_), channel_id=1, source_target_pairs={{0,8},{2,10},{4,28},{6,30},{8,16},{10,18},{12,4},{14,6},{16,24},{1... | collective-permute-start | bytes 786440 | tf_op jit(solution)/shard_map/ppermute | solution.py:211
  13.3 2.4 %collective-permute-start.1 = (bf16[1024,128]{1,0:T(8,128)(2,1)S(1)}, bf16[1024,128]{1,0:T(8,128)(2,1)S(1)}, u32[]{:S(2)}, u32[]{:S(2)}) collective-permute-start(bf16[1024,128]{1,0:T(8,128)(2,1)S(1)} %collective-permute-done.rest_0_), channel_id=1, source_target_pairs={{0,2},{2,0},{4,6},{6,4},{8,10},{10,8},{12,14},{14,12},{16,18},{18,... | collective-permute-start | bytes 786440 | tf_op jit(solution)/shard_map/ppermute | solution.py:214
  14.1 10.8 %collective-permute-start.6 = (bf16[1024,128]{1,0:T(8,128)(2,1)S(1)}, bf16[1024,128]{1,0:T(8,128)(2,1)S(1)}, u32[]{:S(2)}, u32[]{:S(2)}) collective-permute-start(bf16[1024,128]{1,0:T(8,128)(2,1)S(1)} %collective-permute-done.rest_0_), channel_id=1, source_target_pairs={{0,1},{1,0},{2,3},{3,2},{4,5},{5,4},{6,7},{7,6},{8,9},{9,8},{10,11... | collective-permute-start | bytes 786440 | tf_op jit(solution)/shard_map/ppermute | solution.py:251
  21.3 7.2 %collective-permute-start.8 = (bf16[1024,128]{1,0:T(8,128)(2,1)S(1)}, bf16[1024,128]{1,0:T(8,128)(2,1)S(1)}, u32[]{:S(2)}, u32[]{:S(2)}) collective-permute-start(bf16[1024,128]{1,0:T(8,128)(2,1)S(1)} %collective-permute-done.7.rest_2_), channel_id=1, source_target_pairs={{0,1},{1,0},{2,3},{3,2},{4,5},{5,4},{6,7},{7,6},{8,9},{9,8},{10,11... | collective-permute-start | bytes 786440 | tf_op jit(solution)/shard_map/ppermute | solution.py:251
  24.2 13.0 %collective-permute-start.5 = (bf16[2048,128]{1,0:T(8,128)(2,1)S(1)}, bf16[2048,128]{1,0:T(8,128)(2,1)S(1)}, u32[]{:S(2)}, u32[]{:S(2)}) collective-permute-start(bf16[2048,128]{1,0:T(8,128)(2,1)S(1)} %collective-permute-done.4.rest_0_.rest_8_), channel_id=1, source_target_pairs={{0,8},{2,10},{4,0},{6,2},{8,16},{10,18},{12,4},{14,6},{16,24},{18,... | collective-permute-start | bytes 1572872 | tf_op jit(solution)/shard_map/ppermute | solution.py:277
  24.3 4.3 %collective-permute-start.2 = (f32[8,128]{1,0:T(8,128)S(1)}, f32[8,128]{1,0:T(8,128)S(1)}, u32[]{:S(2)}, u32[]{:S(2)}) collective-permute-start(f32[8,128]{1,0:T(8,128)S(1)} %get-tuple-element.24), channel_id=1, source_target_pairs={{0,1},{1,0},{2,3},{3,2},{4,5},{5,4},{6,7},{7,6},{8,9},{9,8},{10,11... | collective-permute-start | bytes 12296 | tf_op jit(solution)/shard_map/ppermute | solution.py:251
  24.9 4.2 %collective-permute-start.9 = (bf16[1024,128]{1,0:T(8,128)(2,1)S(1)}, bf16[1024,128]{1,0:T(8,128)(2,1)S(1)}, u32[]{:S(2)}, u32[]{:S(2)}) collective-permute-start(bf16[1024,128]{1,0:T(8,128)(2,1)S(1)} %collective-permute-done.6.rest_1_), channel_id=1, source_target_pairs={{0,2},{2,0},{4,6},{6,4},{8,10},{10,8},{12,14},{14,12},{16,18},{18,... | collective-permute-start | bytes 786440 | tf_op jit(solution)/shard_map/ppermute | solution.py:214
  28.6 1.5 %collective-permute-start.10 = (bf16[1024,128]{1,0:T(8,128)(2,1)S(1)}, bf16[1024,128]{1,0:T(8,128)(2,1)S(1)}, u32[]{:S(2)}, u32[]{:S(2)}) collective-permute-start(bf16[1024,128]{1,0:T(8,128)(2,1)S(1)} %collective-permute-done.7.rest_2_), channel_id=1, source_target_pairs={{0,2},{2,0},{4,6},{6,4},{8,10},{10,8},{12,14},{14,12},{16,18},{18,... | collective-permute-start | bytes 786440 | tf_op jit(solution)/shard_map/ppermute | solution.py:214
  28.6 1.9 %collective-permute-start.11 = (bf16[1024,128]{1,0:T(8,128)(2,1)S(1)}, bf16[1024,128]{1,0:T(8,128)(2,1)S(1)}, u32[]{:S(2)}, u32[]{:S(2)}) collective-permute-start(bf16[1024,128]{1,0:T(8,128)(2,1)S(1)} %collective-permute-done.8.rest_3_), channel_id=1, source_target_pairs={{0,2},{2,0},{4,6},{6,4},{8,10},{10,8},{12,14},{14,12},{16,18},{18,... | collective-permute-start | bytes 786440 | tf_op jit(solution)/shard_map/ppermute | solution.py:214
  33.4 5.8 %collective-permute-start.12 = (bf16[2048,128]{1,0:T(8,128)(2,1)S(1)}, bf16[2048,128]{1,0:T(8,128)(2,1)S(1)}, u32[]{:S(2)}, u32[]{:S(2)}) collective-permute-start(bf16[2048,128]{1,0:T(8,128)(2,1)S(1)} %collective-permute-done.4.rest_0_.rest_8_), channel_id=1, source_target_pairs={{0,2},{2,0},{4,6},{6,4},{8,10},{10,8},{12,14},{14,12},{16,18},{18,... | collective-permute-start | bytes 1572872 | tf_op jit(solution)/shard_map/ppermute | solution.py:214
  33.6 9.2 %collective-permute-start.16 = (bf16[1024,128]{1,0:T(8,128)(2,1)S(1)}, bf16[1024,128]{1,0:T(8,128)(2,1)S(1)}, u32[]{:S(2)}, u32[]{:S(2)}) collective-permute-start(bf16[1024,128]{1,0:T(8,128)(2,1)S(1)} %shard_map.76), channel_id=1, source_target_pairs={{0,1},{1,0},{2,3},{3,2},{4,5},{5,4},{6,7},{7,6},{8,9},{9,8},{10,11... | collective-permute-start | bytes 786440 | tf_op jit(solution)/shard_map/ppermute | solution.py:251
  37.2 2.0 %collective-permute-start.14 = (bf16[768,128]{1,0:T(8,128)(2,1)S(1)}, bf16[768,128]{1,0:T(8,128)(2,1)S(1)}, u32[]{:S(2)}, u32[]{:S(2)}) collective-permute-start(bf16[768,128]{1,0:T(8,128)(2,1)S(1)} %get-tuple-element.39), channel_id=1, source_target_pairs={{0,2},{2,0},{4,6},{6,4},{8,10},{10,8},{12,14},{14,12},{16,18},{18,... | collective-permute-start | bytes 589832 | tf_op jit(solution)/shard_map/ppermute | solution.py:214
  37.3 1.9 %collective-permute-start.13 = (bf16[768,128]{1,0:T(8,128)(2,1)S(1)}, bf16[768,128]{1,0:T(8,128)(2,1)S(1)}, u32[]{:S(2)}, u32[]{:S(2)}) collective-permute-start(bf16[768,128]{1,0:T(8,128)(2,1)S(1)} %get-tuple-element.40), channel_id=1, source_target_pairs={{0,2},{2,0},{4,6},{6,4},{8,10},{10,8},{12,14},{14,12},{16,18},{18,... | collective-permute-start | bytes 589832 | tf_op jit(solution)/shard_map/ppermute | solution.py:214
  37.8 12.9 %copy-start.2 = (bf16[256,256]{1,0:T(8,128)(2,1)S(1)}, bf16[256,256]{1,0:T(8,128)(2,1)}, u32[]{:S(2)}) copy-start(bf16[256,256]{1,0:T(8,128)(2,1)} %w_neigh.1) | copy-start | bytes 393220
  37.8 1.4 %collective-permute-start.15 = (bf16[512,128]{1,0:T(8,128)(2,1)S(1)}, bf16[512,128]{1,0:T(8,128)(2,1)S(1)}, u32[]{:S(2)}, u32[]{:S(2)}) collective-permute-start(bf16[512,128]{1,0:T(8,128)(2,1)S(1)} %slice.15), channel_id=1, source_target_pairs={{0,2},{2,0},{4,6},{6,4},{8,10},{10,8},{12,14},{14,12},{16,18},{18,... | collective-permute-start | bytes 393224 | tf_op jit(solution)/shard_map/ppermute | solution.py:214
  42.8 7.8 %collective-permute-start.17 = (bf16[1024,128]{1,0:T(8,128)(2,1)S(1)}, bf16[1024,128]{1,0:T(8,128)(2,1)S(1)}, u32[]{:S(2)}, u32[]{:S(2)}) collective-permute-start(bf16[1024,128]{1,0:T(8,128)(2,1)S(1)} %shard_map.77), channel_id=1, source_target_pairs={{0,1},{1,0},{2,3},{3,2},{4,5},{5,4},{6,7},{7,6},{8,9},{9,8},{10,11... | collective-permute-start | bytes 786440 | tf_op jit(solution)/shard_map/ppermute | solution.py:251

commit v4 on v3

--- a/solution.py
+++ b/solution.py
@@ -152,22 +152,26 @@
                 out[i * edge : (i + 1) * edge, :] = acc[:, k * part : (k + 1) * part].astype(out.dtype)
 
 
-def final_kernel(degree, degree_far, base, own0, far0, own1, far1, w_neigh, out):
+def middle_kernel(degree, degree_far, base, own0, far0, w_neigh, mixed, column):
     rows, edge = degree.shape
+    part = own0.shape[1]
     for i in range(rows):
         total = degree[i : i + 1, :] + degree_far[i : i + 1, :]
         scale = 1.0 / jnp.maximum(total, 1.0)
-        column = jnp.broadcast_to(scale, (edge, edge)).T
         cut = pl.ds(i * edge, edge)
-        mean = jnp.concatenate(
-            [
-                ((own0[cut, :] + far0[cut, :].astype(jnp.float32)) * column).astype(jnp.bfloat16),
-                ((own1[cut, :] + far1[cut, :].astype(jnp.float32)) * column).astype(jnp.bfloat16),
-            ],
-            axis=1,
-        )
-        mixed = base[cut, :] + jnp.dot(mean, w_neigh[...], preferred_element_type=jnp.float32)
-        out[cut, :] = jnp.maximum(mixed, 0.0).astype(out.dtype)
+        column[cut, :] = jnp.broadcast_to(scale, (edge, edge)).T
+        mean = ((own0[cut, :] + far0[cut, :].astype(jnp.float32)) * column[cut, :]).astype(jnp.bfloat16)
+        mixed[cut, :] = base[cut, :] + jnp.dot(mean, w_neigh[:part, :], preferred_element_type=jnp.float32)
+
+
+def final_kernel(column, mixed, own1, far1, w_neigh, out):
+    edge = column.shape[1]
+    part = own1.shape[1]
+    for i in range(column.shape[0] // edge):
+        cut = pl.ds(i * edge, edge)
+        mean = ((own1[cut, :] + far1[cut, :].astype(jnp.float32)) * column[cut, :]).astype(jnp.bfloat16)
+        total = mixed[cut, :] + jnp.dot(mean, w_neigh[part:, :], preferred_element_type=jnp.float32)
+        out[cut, :] = jnp.maximum(total, 0.0).astype(out.dtype)
 
 
 def local(features, adjacency, columns, live, w_self, w_neigh, bias):
@@ -296,14 +300,22 @@
     nearby = product_of(True, (0, 1), adjacency, after(features, far1), pair, *half0, *half1)
     far = (other0, other1)
 
+    mixed, column = pl.pallas_call(
+        middle_kernel,
+        out_shape=[jax.ShapeDtypeStruct((out_rows, n), jnp.float32) for n in (width, edge)],
+        in_specs=[vmem] * 6,
+        out_specs=[vmem] * 2,
+        compiler_params=params,
+        cost_estimate=TINY,
+    )(degree, degree_far, base, nearby[0], far[0], w_neigh)
     return pl.pallas_call(
         final_kernel,
         out_shape=jax.ShapeDtypeStruct((out_rows, width), jnp.bfloat16),
-        in_specs=[vmem] * 8,
+        in_specs=[vmem] * 5,
         out_specs=vmem,
         compiler_params=params,
         cost_estimate=TINY,
-    )(degree, degree_far, base, nearby[0], far[0], nearby[1], far[1], w_neigh)
+    )(column, mixed, nearby[1], far[1], w_neigh)
 
 
 def solution(mesh):

time: 52.1 us -> 52.4 us (level)
  transfers between devices with their start and end apart: 18 -> 18, of which waited for: 8 -> 7; matrix products, arithmetic and copies ran while one was open for 7% -> 7% of each run, Pallas kernels for 42% -> 43%
where the time goes in v4:
time: 52.4 us; the launch traced here: 52.1 us
  Pallas kernels  23.3 us (44%)
  starting transfers between devices  13.3 us (25%)
  waiting for transfers between devices  10.9 us (21%)
  local copies, waits for them, and re-layouts  2.89 us (6%)
  other arithmetic  1.5 us (3%)
    pallas_call x3, Pallas kernels, product_of(): pl.pallas_call(functools.partial(product_kernel, own_part, halves, reside...  12.7 us
    pallas_call x2, Pallas kernels, degree_of(): pl.pallas_call(functools.partial(degree_kernel, own_part), out_shape=[sha...  7.8 us
    ppermute x5, starting transfers between devices, rep_swap(): return lax.ppermute(x, 'rep', [(0, 1), (1, 0)])  6.6 us
    ppermute x5, waiting for transfers between devices, rep_swap(): return lax.ppermute(x, 'rep', [(0, 1), (1, 0)])  3.75 us
    ppermute x2, starting transfers between devices, cross_of(): return lax.ppermute(sent, 'row', swap_route(count, 2))  3.1 us
    ppermute x8, waiting for transfers between devices, over(): return lax.ppermute(p, 'row', swap_route(count, 1))  2.67 us
    ppermute x1, starting transfers between devices, ahead_of(): return lax.ppermute(p, 'row', ahead_route(count))  2.14 us
    ppermute x1, waiting for transfers between devices, loop_of(): return lax.ppermute(p, 'row', loop_route(count))  2.09 us
  transfers between devices with their start and end apart: 18, of which 7 were waited for; matrix products, arithmetic and copies ran while one was open for 7% of the time, Pallas kernels for 43%

profile of v4, /device:TPU:0, one launch (start us, length us, event | category | flops | bytes accessed | tf_op | source)
XLA Modules:
  0.0 52.1 jit_solution(9361330450832102935)
XLA Ops:
  0.0 1.0 %constant_dynamic-slice_fusion = bf16[1024,128]{1,0:T(8,128)(2,1)S(1)} fusion(bf16[2048,256]{1,0:T(8,128)(2,1)} %feats.4, s32[]{:T(128)S(6)} %select_n.51), kind=kLoop, calls=%fused_computation.13 | loop fusion | bytes 524292 | tf_op jit(solution)/shard_map/dynamic_slice | solution.py:206
  1.0 3.0 %collective-permute-start = (bf16[1024,128]{1,0:T(8,128)(2,1)S(1)}, bf16[1024,128]{1,0:T(8,128)(2,1)S(1)}, u32[]{:S(2)}, u32[]{:S(2)}) collective-permute-start(bf16[1024,128]{1,0:T(8,128)(2,1)S(1)} %constant_dynamic-slice_fusion), channel_id=1, source_target_pairs={{0,4},{2,6},{4,0},{6,2},{8,12},{10,14},{12,8},{14,10},{16,20},{18,... | collective-permute-start | bytes 786440 | tf_op jit(solution)/shard_map/ppermute | solution.py:204
  4.0 1.9 %slice.12 = bf16[2048,128]{1,0:T(8,128)(2,1)} slice(bf16[2048,256]{1,0:T(8,128)(2,1)} %feats.4), slice={[0:2048], [128:256]} | slice | bytes 1048576 | tf_op jit(solution)/shard_map/slice | solution.py:207
  5.9 0.7 %subtract_clamp_fusion.usable = s32[16]{0:T(128)S(1)} fusion(s32[16]{0:T(128)} %param.10, s32[]{:T(128)S(6)} %mul.13), kind=kLoop, calls=%fused_computation.12 | loop fusion | flops 32 | bytes 132 | tf_op jit(solution)/shard_map/jit(clip)/min | solution.py:186
  6.6 3.9 %shard_map.73.degree = f32[8,128]{1,0:T(8,128)S(1)} custom-call(s32[16]{0:T(128)S(1)} %subtract_clamp_fusion.usable, s32[1]{0:T(128)} %bitcast.place, bf16[16,24,128,128]{3,2,1,0:T(8,128)(2,1)} %adj.5), custom_call_target="tpu_custom_call" | custom-call | tf_op jit(solution)/shard_map/pallas_call | solution.py:226
  10.5 0.6 %collective-permute-done.rest_0_ = bf16[1024,128]{1,0:T(8,128)(2,1)S(1)} collective-permute-done((bf16[1024,128]{1,0:T(8,128)(2,1)S(1)}, bf16[1024,128]{1,0:T(8,128)(2,1)S(1)}, u32[]{:S(2)}, u32[]{:S(2)}) %collective-permute-start) | collective-permute-done | bytes 262176 | tf_op jit(solution)/shard_map/ppermute | solution.py:204
  11.1 2.1 %collective-permute-start.7 = (bf16[1024,128]{1,0:T(8,128)(2,1)S(1)}, bf16[1024,128]{1,0:T(8,128)(2,1)S(1)}, u32[]{:S(2)}, u32[]{:S(2)}) collective-permute-start(bf16[1024,128]{1,0:T(8,128)(2,1)S(1)} %collective-permute-done.rest_0_), channel_id=1, source_target_pairs={{0,8},{2,10},{4,28},{6,30},{8,16},{10,18},{12,4},{14,6},{16,24},{1... | collective-permute-start | bytes 786440 | tf_op jit(solution)/shard_map/ppermute | solution.py:215
  13.3 0.8 %fusion.2.index = s32[16,24]{1,0:T(8,128)S(1)} fusion(s32[16,24]{1,0:T(8,128)} %param.9, s32[]{:T(128)S(6)} %neg.7, s32[]{:T(128)S(6)} %sub.26, s32[]{:T(128)S(6)} %neg.6, s32[]{:T(128)S(6)} %select_n.54, s32[]{:T(128)S(6)} %axis_index.25, s32[16]{0:T(128)S(1)} %subtract_clamp_fusion.usable), kind=kLoop, calls=%fused_computation.7 | loop fusion | flops 12288 | bytes 3156 | tf_op jit(solution)/shard_map/jit(_where)/select_n | solution.py:196
  14.1 1.5 %collective-permute-start.6 = (bf16[1024,128]{1,0:T(8,128)(2,1)S(1)}, bf16[1024,128]{1,0:T(8,128)(2,1)S(1)}, u32[]{:S(2)}, u32[]{:S(2)}) collective-permute-start(bf16[1024,128]{1,0:T(8,128)(2,1)S(1)} %collective-permute-done.rest_0_), channel_id=1, source_target_pairs={{0,1},{1,0},{2,3},{3,2},{4,5},{5,4},{6,7},{7,6},{8,9},{9,8},{10,11... | collective-permute-start | bytes 786440 | tf_op jit(solution)/shard_map/ppermute | solution.py:255
  15.6 3.9 %shard_map.74 = (f32[8,128]{1,0:T(8,128)S(1)}, bf16[8,24,128,128]{3,2,1,0:T(8,128)(2,1)S(1)}) custom-call(s32[16]{0:T(128)S(1)} %subtract_clamp_fusion.usable, s32[1]{0:T(128)} %bitcast.place, bf16[16,24,128,128]{3,2,1,0:T(8,128)(2,1)} %adj.5), custom_call_target="tpu_custom_call" | custom-call | tf_op jit(solution)/shard_map/pallas_call | solution.py:226
  19.5 1.8 %collective-permute-done.7.rest_2_ = bf16[1024,128]{1,0:T(8,128)(2,1)S(1)} collective-permute-done((bf16[1024,128]{1,0:T(8,128)(2,1)S(1)}, bf16[1024,128]{1,0:T(8,128)(2,1)S(1)}, u32[]{:S(2)}, u32[]{:S(2)}) %collective-permute-start.7) | collective-permute-done | bytes 262176 | tf_op jit(solution)/shard_map/ppermute | solution.py:215
  21.3 1.5 %collective-permute-start.8 = (bf16[1024,128]{1,0:T(8,128)(2,1)S(1)}, bf16[1024,128]{1,0:T(8,128)(2,1)S(1)}, u32[]{:S(2)}, u32[]{:S(2)}) collective-permute-start(bf16[1024,128]{1,0:T(8,128)(2,1)S(1)} %collective-permute-done.7.rest_2_), channel_id=1, source_target_pairs={{0,1},{1,0},{2,3},{3,2},{4,5},{5,4},{6,7},{7,6},{8,9},{9,8},{10,11... | collective-permute-start | bytes 786440 | tf_op jit(solution)/shard_map/ppermute | solution.py:255
  22.9 1.3 %shard_map.75.base = f32[1024,256]{1,0:T(8,128)S(1)} custom-call(s32[1]{0:T(128)} %bitcast.place, bf16[2048,256]{1,0:T(8,128)(2,1)} %feats.4, bf16[256,256]{1,0:T(8,128)(2,1)S(1)} %copy-done.2, f32[1,256]{1,0:T(1,128)S(1)} %bitcast.3), custom_call_target="tpu_custom_call" | custom-call | tf_op jit(solution)/shard_map/pallas_call | solution.py:258
  24.3 0.6 %collective-permute-start.2 = (f32[8,128]{1,0:T(8,128)S(1)}, f32[8,128]{1,0:T(8,128)S(1)}, u32[]{:S(2)}, u32[]{:S(2)}) collective-permute-start(f32[8,128]{1,0:T(8,128)S(1)} %get-tuple-element.26), channel_id=1, source_target_pairs={{0,1},{1,0},{2,3},{3,2},{4,5},{5,4},{6,7},{7,6},{8,9},{9,8},{10,11... | collective-permute-start | bytes 12296 | tf_op jit(solution)/shard_map/ppermute | solution.py:255
  24.9 3.7 %collective-permute-done.8.rest_3_ = bf16[1024,128]{1,0:T(8,128)(2,1)S(1)} collective-permute-done((bf16[1024,128]{1,0:T(8,128)(2,1)S(1)}, bf16[1024,128]{1,0:T(8,128)(2,1)S(1)}, u32[]{:S(2)}, u32[]{:S(2)}) %collective-permute-start.8) | collective-permute-done | bytes 262176 | tf_op jit(solution)/shard_map/ppermute | solution.py:255
  29.1 1.0 %collective-permute-done.10.rest_6_ = bf16[1024,128]{1,0:T(8,128)(2,1)S(1)} collective-permute-done((bf16[1024,128]{1,0:T(8,128)(2,1)S(1)}, bf16[1024,128]{1,0:T(8,128)(2,1)S(1)}, u32[]{:S(2)}, u32[]{:S(2)}) %collective-permute-start.10) | collective-permute-done | bytes 262176 | tf_op jit(solution)/shard_map/ppermute | solution.py:218
  30.5 2.9 %shard_map.76 = bf16[1024,128]{1,0:T(8,128)(2,1)S(1)} custom-call(s32[16,24]{1,0:T(8,128)S(1)} %fusion.2.index, s32[2]{0:T(128)S(1)} %pad_add_fusion.place, bf16[8,24,128,128]{3,2,1,0:T(8,128)(2,1)S(1)} %get-tuple-element.28.adj, bf16[2048,256]{1,0:T(8,128)(2,1)S(1)} %copy-done, bf16[2048,256]{1,0:T(8,128)(2,1)S(1)} %collective-permute-done.3.pair, ...), custom_call_target="tpu_custom_call" | custom-call | tf_op jit(solution)/shard_map/pallas_call | solution.py:239
  33.6 1.5 %collective-permute-start.16 = (bf16[1024,128]{1,0:T(8,128)(2,1)S(1)}, bf16[1024,128]{1,0:T(8,128)(2,1)S(1)}, u32[]{:S(2)}, u32[]{:S(2)}) collective-permute-start(bf16[1024,128]{1,0:T(8,128)(2,1)S(1)} %shard_map.76), channel_id=1, source_target_pairs={{0,1},{1,0},{2,3},{3,2},{4,5},{5,4},{6,7},{7,6},{8,9},{9,8},{10,11... | collective-permute-start | bytes 786440 | tf_op jit(solution)/shard_map/ppermute | solution.py:255
  35.1 2.1 %collective-permute-done.5.rest_1_.rest_9_ = bf16[2048,128]{1,0:T(8,128)(2,1)S(1)} collective-permute-done((bf16[2048,128]{1,0:T(8,128)(2,1)S(1)}, bf16[2048,128]{1,0:T(8,128)(2,1)S(1)}, u32[]{:S(2)}, u32[]{:S(2)}) %collective-permute-start.5) | collective-permute-done | bytes 524320 | tf_op jit(solution)/shard_map/ppermute | solution.py:281
  37.9 1.3 %collective-permute-done.15.rest_5_.rest_13_ = bf16[512,128]{1,0:T(8,128)(2,1)S(1)} collective-permute-done((bf16[512,128]{1,0:T(8,128)(2,1)S(1)}, bf16[512,128]{1,0:T(8,128)(2,1)S(1)}, u32[]{:S(2)}, u32[]{:S(2)}) %collective-permute-start.15) | collective-permute-done | bytes 131104 | tf_op jit(solution)/shard_map/ppermute | solution.py:218
  39.2 3.6 %shard_map.77 = bf16[1024,128]{1,0:T(8,128)(2,1)S(1)} custom-call(s32[16,24]{1,0:T(8,128)S(1)} %fusion.2.index, s32[2]{0:T(128)S(1)} %pad_add_fusion.place, bf16[8,24,128,128]{3,2,1,0:T(8,128)(2,1)S(1)} %get-tuple-element.28.adj, bf16[2048,256]{1,0:T(8,128)(2,1)S(1)} %copy-done, bf16[2048,256]{1,0:T(8,128)(2,1)S(1)} %collective-permute-done.3.pair, ...), custom_call_target="tpu_custom_call" | custom-call | tf_op jit(solution)/shard_map/pallas_call | solution.py:239
  42.8 1.5 %collective-permute-start.17 = (bf16[1024,128]{1,0:T(8,128)(2,1)S(1)}, bf16[1024,128]{1,0:T(8,128)(2,1)S(1)}, u32[]{:S(2)}, u32[]{:S(2)}) collective-permute-start(bf16[1024,128]{1,0:T(8,128)(2,1)S(1)} %shard_map.77), channel_id=1, source_target_pairs={{0,1},{1,0},{2,3},{3,2},{4,5},{5,4},{6,7},{7,6},{8,9},{9,8},{10,11... | collective-permute-start | bytes 786440 | tf_op jit(solution)/shard_map/ppermute | solution.py:255
  44.3 6.2 %shard_map.78 = (f32[1024,128]{1,0:T(8,128)S(1)}, f32[1024,128]{1,0:T(8,128)S(1)}) custom-call(s32[16,24]{1,0:T(8,128)S(1)} %fusion.2.index, s32[2]{0:T(128)S(1)} %pad_add_fusion.place, bf16[16,24,128,128]{3,2,1,0:T(8,128)(2,1)} %adj.5, bf16[2048,256]{1,0:T(8,128)(2,1)S(1)} %copy-done, bf16[2048,256]{1,0:T(8,128)(2,1)S(1)} %collective-permute-done.3.pair, ...), custom_call_target="tpu_custom_call" | custom-call | tf_op jit(solution)/shard_map/pallas_call | solution.py:239
  51.0 1.1 %shard_map.80 = bf16[1024,256]{1,0:T(8,128)(2,1)} custom-call(f32[1024,128]{1,0:T(8,128)S(1)} %get-tuple-element.39.column, f32[1024,256]{1,0:T(8,128)S(1)} %get-tuple-element.40.mixed, f32[1024,128]{1,0:T(8,128)S(1)} %get-tuple-element.41.own1, bf16[1024,128]{1,0:T(8,128)(2,1)S(1)} %collective-permute-done.17.far1, bf16[256,256]{1,0:T(8,128)(2,1)S(1)} %copy-done.1), custom_call_target="tpu_custom_call" | custom-call | tf_op jit(solution)/shard_map/pallas_call | solution.py:311
  (35 shorter events, 2.5 us)
Async XLA Ops:
  1.0 10.1 %collective-permute-start = (bf16[1024,128]{1,0:T(8,128)(2,1)S(1)}, bf16[1024,128]{1,0:T(8,128)(2,1)S(1)}, u32[]{:S(2)}, u32[]{:S(2)}) collective-permute-start(bf16[1024,128]{1,0:T(8,128)(2,1)S(1)} %constant_dynamic-slice_fusion), channel_id=1, source_target_pairs={{0,4},{2,6},{4,0},{6,2},{8,12},{10,14},{12,8},{14,10},{16,20},{18,... | collective-permute-start | bytes 786440 | tf_op jit(solution)/shard_map/ppermute | solution.py:204
  4.0 26.1 %collective-permute-start.3 = (bf16[2048,256]{1,0:T(8,128)(2,1)}, bf16[2048,256]{1,0:T(8,128)(2,1)S(1)}, u32[]{:S(2)}, u32[]{:S(2)}) collective-permute-start(bf16[2048,256]{1,0:T(8,128)(2,1)} %feats.4), channel_id=1, source_target_pairs={{0,2},{2,0},{4,6},{6,4},{8,10},{10,8},{12,14},{14,12},{16,18},{18,... | collective-permute-start | bytes 3145736 | tf_op jit(solution)/shard_map/ppermute | solution.py:208
  5.8 18.4 %collective-permute-start.4 = (bf16[2048,128]{1,0:T(8,128)(2,1)}, bf16[2048,128]{1,0:T(8,128)(2,1)S(1)}, u32[]{:S(2)}, u32[]{:S(2)}) collective-permute-start(bf16[2048,128]{1,0:T(8,128)(2,1)} %slice.12), channel_id=1, source_target_pairs={{0,4},{2,6},{4,0},{6,2},{8,12},{10,14},{12,8},{14,10},{16,20},{18,... | collective-permute-start | bytes 1572872 | tf_op jit(solution)/shard_map/ppermute | solution.py:204
  6.6 16.2 %copy-start.2 = (bf16[256,256]{1,0:T(8,128)(2,1)S(1)}, bf16[256,256]{1,0:T(8,128)(2,1)}, u32[]{:S(2)}) copy-start(bf16[256,256]{1,0:T(8,128)(2,1)} %w_self.1) | copy-start | bytes 393220
  6.6 16.3 %copy-start.3 = (f32[256]{0:T(256)S(1)}, f32[256]{0:T(256)}, u32[]{:S(2)}) copy-start(f32[256]{0:T(256)} %param.13) | copy-start | bytes 3076
  6.6 23.9 %copy-start = (bf16[2048,256]{1,0:T(8,128)(2,1)S(1)}, bf16[2048,256]{1,0:T(8,128)(2,1)}, u32[]{:S(2)}) copy-start(bf16[2048,256]{1,0:T(8,128)(2,1)} %feats.4) | copy-start | bytes 3145732
  11.1 10.2 %collective-permute-start.7 = (bf16[1024,128]{1,0:T(8,128)(2,1)S(1)}, bf16[1024,128]{1,0:T(8,128)(2,1)S(1)}, u32[]{:S(2)}, u32[]{:S(2)}) collective-permute-start(bf16[1024,128]{1,0:T(8,128)(2,1)S(1)} %collective-permute-done.rest_0_), channel_id=1, source_target_pairs={{0,8},{2,10},{4,28},{6,30},{8,16},{10,18},{12,4},{14,6},{16,24},{1... | collective-permute-start | bytes 786440 | tf_op jit(solution)/shard_map/ppermute | solution.py:215
  13.3 2.4 %collective-permute-start.1 = (bf16[1024,128]{1,0:T(8,128)(2,1)S(1)}, bf16[1024,128]{1,0:T(8,128)(2,1)S(1)}, u32[]{:S(2)}, u32[]{:S(2)}) collective-permute-start(bf16[1024,128]{1,0:T(8,128)(2,1)S(1)} %collective-permute-done.rest_0_), channel_id=1, source_target_pairs={{0,2},{2,0},{4,6},{6,4},{8,10},{10,8},{12,14},{14,12},{16,18},{18,... | collective-permute-start | bytes 786440 | tf_op jit(solution)/shard_map/ppermute | solution.py:218
  14.1 10.8 %collective-permute-start.6 = (bf16[1024,128]{1,0:T(8,128)(2,1)S(1)}, bf16[1024,128]{1,0:T(8,128)(2,1)S(1)}, u32[]{:S(2)}, u32[]{:S(2)}) collective-permute-start(bf16[1024,128]{1,0:T(8,128)(2,1)S(1)} %collective-permute-done.rest_0_), channel_id=1, source_target_pairs={{0,1},{1,0},{2,3},{3,2},{4,5},{5,4},{6,7},{7,6},{8,9},{9,8},{10,11... | collective-permute-start | bytes 786440 | tf_op jit(solution)/shard_map/ppermute | solution.py:255
  21.3 7.2 %collective-permute-start.8 = (bf16[1024,128]{1,0:T(8,128)(2,1)S(1)}, bf16[1024,128]{1,0:T(8,128)(2,1)S(1)}, u32[]{:S(2)}, u32[]{:S(2)}) collective-permute-start(bf16[1024,128]{1,0:T(8,128)(2,1)S(1)} %collective-permute-done.7.rest_2_), channel_id=1, source_target_pairs={{0,1},{1,0},{2,3},{3,2},{4,5},{5,4},{6,7},{7,6},{8,9},{9,8},{10,11... | collective-permute-start | bytes 786440 | tf_op jit(solution)/shard_map/ppermute | solution.py:255
  24.2 13.0 %collective-permute-start.5 = (bf16[2048,128]{1,0:T(8,128)(2,1)S(1)}, bf16[2048,128]{1,0:T(8,128)(2,1)S(1)}, u32[]{:S(2)}, u32[]{:S(2)}) collective-permute-start(bf16[2048,128]{1,0:T(8,128)(2,1)S(1)} %collective-permute-done.4.rest_0_.rest_8_), channel_id=1, source_target_pairs={{0,8},{2,10},{4,0},{6,2},{8,16},{10,18},{12,4},{14,6},{16,24},{18,... | collective-permute-start | bytes 1572872 | tf_op jit(solution)/shard_map/ppermute | solution.py:281
  24.3 4.3 %collective-permute-start.2 = (f32[8,128]{1,0:T(8,128)S(1)}, f32[8,128]{1,0:T(8,128)S(1)}, u32[]{:S(2)}, u32[]{:S(2)}) collective-permute-start(f32[8,128]{1,0:T(8,128)S(1)} %get-tuple-element.26), channel_id=1, source_target_pairs={{0,1},{1,0},{2,3},{3,2},{4,5},{5,4},{6,7},{7,6},{8,9},{9,8},{10,11... | collective-permute-start | bytes 12296 | tf_op jit(solution)/shard_map/ppermute | solution.py:255
  24.9 4.2 %collective-permute-start.9 = (bf16[1024,128]{1,0:T(8,128)(2,1)S(1)}, bf16[1024,128]{1,0:T(8,128)(2,1)S(1)}, u32[]{:S(2)}, u32[]{:S(2)}) collective-permute-start(bf16[1024,128]{1,0:T(8,128)(2,1)S(1)} %collective-permute-done.6.rest_1_), channel_id=1, source_target_pairs={{0,2},{2,0},{4,6},{6,4},{8,10},{10,8},{12,14},{14,12},{16,18},{18,... | collective-permute-start | bytes 786440 | tf_op jit(solution)/shard_map/ppermute | solution.py:218
  28.6 1.5 %collective-permute-start.10 = (bf16[1024,128]{1,0:T(8,128)(2,1)S(1)}, bf16[1024,128]{1,0:T(8,128)(2,1)S(1)}, u32[]{:S(2)}, u32[]{:S(2)}) collective-permute-start(bf16[1024,128]{1,0:T(8,128)(2,1)S(1)} %collective-permute-done.7.rest_2_), channel_id=1, source_target_pairs={{0,2},{2,0},{4,6},{6,4},{8,10},{10,8},{12,14},{14,12},{16,18},{18,... | collective-permute-start | bytes 786440 | tf_op jit(solution)/shard_map/ppermute | solution.py:218
  28.6 1.9 %collective-permute-start.11 = (bf16[1024,128]{1,0:T(8,128)(2,1)S(1)}, bf16[1024,128]{1,0:T(8,128)(2,1)S(1)}, u32[]{:S(2)}, u32[]{:S(2)}) collective-permute-start(bf16[1024,128]{1,0:T(8,128)(2,1)S(1)} %collective-permute-done.8.rest_3_), channel_id=1, source_target_pairs={{0,2},{2,0},{4,6},{6,4},{8,10},{10,8},{12,14},{14,12},{16,18},{18,... | collective-permute-start | bytes 786440 | tf_op jit(solution)/shard_map/ppermute | solution.py:218
  33.4 5.8 %collective-permute-start.12 = (bf16[2048,128]{1,0:T(8,128)(2,1)S(1)}, bf16[2048,128]{1,0:T(8,128)(2,1)S(1)}, u32[]{:S(2)}, u32[]{:S(2)}) collective-permute-start(bf16[2048,128]{1,0:T(8,128)(2,1)S(1)} %collective-permute-done.4.rest_0_.rest_8_), channel_id=1, source_target_pairs={{0,2},{2,0},{4,6},{6,4},{8,10},{10,8},{12,14},{14,12},{16,18},{18,... | collective-permute-start | bytes 1572872 | tf_op jit(solution)/shard_map/ppermute | solution.py:218
  33.6 9.2 %collective-permute-start.16 = (bf16[1024,128]{1,0:T(8,128)(2,1)S(1)}, bf16[1024,128]{1,0:T(8,128)(2,1)S(1)}, u32[]{:S(2)}, u32[]{:S(2)}) collective-permute-start(bf16[1024,128]{1,0:T(8,128)(2,1)S(1)} %shard_map.76), channel_id=1, source_target_pairs={{0,1},{1,0},{2,3},{3,2},{4,5},{5,4},{6,7},{7,6},{8,9},{9,8},{10,11... | collective-permute-start | bytes 786440 | tf_op jit(solution)/shard_map/ppermute | solution.py:255
  37.2 2.0 %collective-permute-start.14 = (bf16[768,128]{1,0:T(8,128)(2,1)S(1)}, bf16[768,128]{1,0:T(8,128)(2,1)S(1)}, u32[]{:S(2)}, u32[]{:S(2)}) collective-permute-start(bf16[768,128]{1,0:T(8,128)(2,1)S(1)} %get-tuple-element.43), channel_id=1, source_target_pairs={{0,2},{2,0},{4,6},{6,4},{8,10},{10,8},{12,14},{14,12},{16,18},{18,... | collective-permute-start | bytes 589832 | tf_op jit(solution)/shard_map/ppermute | solution.py:218
  37.3 1.9 %collective-permute-start.13 = (bf16[768,128]{1,0:T(8,128)(2,1)S(1)}, bf16[768,128]{1,0:T(8,128)(2,1)S(1)}, u32[]{:S(2)}, u32[]{:S(2)}) collective-permute-start(bf16[768,128]{1,0:T(8,128)(2,1)S(1)} %get-tuple-element.44), channel_id=1, source_target_pairs={{0,2},{2,0},{4,6},{6,4},{8,10},{10,8},{12,14},{14,12},{16,18},{18,... | collective-permute-start | bytes 589832 | tf_op jit(solution)/shard_map/ppermute | solution.py:218
  37.8 12.8 %copy-start.1 = (bf16[256,256]{1,0:T(8,128)(2,1)S(1)}, bf16[256,256]{1,0:T(8,128)(2,1)}, u32[]{:S(2)}) copy-start(bf16[256,256]{1,0:T(8,128)(2,1)} %w_neigh.3) | copy-start | bytes 393220
  37.8 1.4 %collective-permute-start.15 = (bf16[512,128]{1,0:T(8,128)(2,1)S(1)}, bf16[512,128]{1,0:T(8,128)(2,1)S(1)}, u32[]{:S(2)}, u32[]{:S(2)}) collective-permute-start(bf16[512,128]{1,0:T(8,128)(2,1)S(1)} %slice.15), channel_id=1, source_target_pairs={{0,2},{2,0},{4,6},{6,4},{8,10},{10,8},{12,14},{14,12},{16,18},{18,... | collective-permute-start | bytes 393224 | tf_op jit(solution)/shard_map/ppermute | solution.py:218
  42.8 8.1 %collective-permute-start.17 = (bf16[1024,128]{1,0:T(8,128)(2,1)S(1)}, bf16[1024,128]{1,0:T(8,128)(2,1)S(1)}, u32[]{:S(2)}, u32[]{:S(2)}) collective-permute-start(bf16[1024,128]{1,0:T(8,128)(2,1)S(1)} %shard_map.77), channel_id=1, source_target_pairs={{0,1},{1,0},{2,3},{3,2},{4,5},{5,4},{6,7},{7,6},{8,9},{9,8},{10,11... | collective-permute-start | bytes 786440 | tf_op jit(solution)/shard_map/ppermute | solution.py:255
